TPU v7x, 32 devices: a whole 2x2x4 slice. The times are simulated.
32 devices in a mesh: head: 4 (over z), wide: 8 (over y, x, core).
Axes of the slice: x: 2, y: 2, z: 4, core: 2. Of those that a mesh axis runs over, the one named last changes fastest.
Arguments:
- residual: bfloat16 [1024, 4096], P('head'), may hold values from -150 to 150
- norm_gain: float32 [4096], replicated, may hold values from 0.5 to 1.5
- w_gate: bfloat16 [4096, 7168], P(None, 'wide'), may hold values from -0.09375 to 0.09375
- w_up: bfloat16 [4096, 7168], P(None, 'wide'), may hold values from -0.09375 to 0.09375
- grad_hidden: bfloat16 [1024, 7168], P('head', 'wide'), may hold values from -4 to 4
- grad_out: bfloat16 [1024, 4096], P('head'), may hold values from -4 to 4
- out_proj: bfloat16 [4096, 4096], P('wide', 'head'), may hold values from -0.09375 to 0.09375
- queries: bfloat16 [1024, 4096], P('wide', 'head'), may hold values from -200 to 200
- keys_in: bfloat16 [1024, 512], P('wide', 'head'), may hold values from -4 to 4
- values_in: bfloat16 [1024, 512], P('wide', 'head'), may hold values from -6 to 6
- doc_ids: int32 [1024], replicated, may hold values from 0 to 3, never falling along the last dimension, each value on 1 to 768 neighbouring positions
Outputs:
- grad_resid: bfloat16 [1024, 4096], P('head')
- grad_gain: float32 [4096], replicated
- grad_gate: bfloat16 [4096, 7168], P('head', 'wide')
- grad_up: bfloat16 [4096, 7168], P('head', 'wide')
- grad_proj: bfloat16 [4096, 4096], P('wide', 'head')
- grad_query: bfloat16 [1024, 4096], P('wide', 'head')
- grad_key: bfloat16 [1024, 512], P('wide', 'head')
- grad_value: bfloat16 [1024, 512], P('wide', 'head')
Inputs may be any that keep to these rules, and one draw needn't show every extreme that they name: `doc_ids`: document ids never fall along the tokens; each document holds at most 768 tokens, and one holds exactly that many.
All inputs are finite; a program needn't handle non-finite values.
Results may differ from a plain program's by a relative error of at most 0.019.
Values may be sent and summed in bfloat16 or wider, within the bound.
A program may use at most 192 MiB of HBM per device.

v0:
```python
import math

import jax
import jax.numpy as jnp
from jax import lax
from jax.sharding import PartitionSpec as P

EPSILON = 1e-05


def local(
    residual,
    norm_gain,
    w_gate,
    w_up,
    grad_hidden,
    grad_out,
    out_proj,
    queries,
    keys_in,
    values_in,
    doc_ids,
):
    heads_n = lax.axis_size("head")
    wide_n = lax.axis_size("wide")
    wide_at = lax.axis_index("wide")
    hidden_dev = w_gate.shape[1]
    contract_last = (((1,), (1,)), ((), ()))
    contract_first = (((0,), (0,)), ((), ()))
    resid_f = residual.astype(jnp.float32)
    inv_rms = lax.rsqrt(jnp.mean(resid_f * resid_f, axis=-1, keepdims=True) + EPSILON)
    normed_f = resid_f * inv_rms
    normed = (normed_f * norm_gain).astype(jnp.bfloat16)
    gate_pre = jnp.dot(normed, w_gate, preferred_element_type=jnp.float32)
    up_pre = jnp.dot(normed, w_up, preferred_element_type=jnp.float32)
    sigma = jax.nn.sigmoid(gate_pre)
    grad_h = grad_hidden.astype(jnp.float32)
    grad_g = (grad_h * up_pre * sigma * (1.0 + gate_pre * (1.0 - sigma))).astype(jnp.bfloat16)
    grad_u = (grad_h * gate_pre * sigma).astype(jnp.bfloat16)
    partial_norm = lax.dot_general(
        grad_g, w_gate, contract_last, preferred_element_type=jnp.float32
    )
    partial_norm = partial_norm + lax.dot_general(
        grad_u, w_up, contract_last, preferred_element_type=jnp.float32
    )
    grad_norm = lax.psum(partial_norm.astype(jnp.bfloat16), "wide").astype(jnp.float32)
    both_grads = jnp.concatenate([grad_g, grad_u], axis=1)
    weight_sums = lax.psum_scatter(
        lax.dot_general(
            normed, both_grads, contract_first, preferred_element_type=jnp.float32
        ).astype(jnp.bfloat16),
        "head",
        scatter_dimension=0,
        tiled=True,
    ).astype(jnp.float32)
    grad_gate = weight_sums[:, :hidden_dev].astype(jnp.bfloat16)
    grad_up = weight_sums[:, hidden_dev:].astype(jnp.bfloat16)
    grad_gain = lax.psum(jnp.sum(grad_norm * normed_f, axis=0), "head")
    scaled = grad_norm * norm_gain
    mean_term = jnp.mean(scaled * normed_f, axis=-1, keepdims=True)
    grad_resid = (grad_out.astype(jnp.float32) + inv_rms * (scaled - normed_f * mean_term)).astype(
        jnp.bfloat16
    )
    tok_att = queries.shape[0]
    head_dim = keys_in.shape[1]
    per_kv = queries.shape[1] // head_dim
    keys_all, values_all = (
        lax.all_gather(keys_in, "wide", axis=0, tiled=True),
        lax.all_gather(values_in, "wide", axis=0, tiled=True),
    )
    tok_total = keys_all.shape[0]
    q_offset = wide_at * tok_att
    positions = jnp.arange(tok_total, dtype=jnp.int32)
    q_pos = q_offset + jnp.arange(tok_att, dtype=jnp.int32)
    q_docs = lax.dynamic_slice_in_dim(doc_ids, q_offset, tok_att, 0)
    visible = (q_docs[:, None] == doc_ids[None, :]) & (positions[None, :] <= q_pos[:, None])
    score_scale = 1.0 / math.sqrt(head_dim)
    query3 = queries.reshape(tok_att, per_kv, head_dim)
    scores = (
        jnp.einsum("thd,sd->hts", query3, keys_all, preferred_element_type=jnp.float32)
        * score_scale
    )
    scores = jnp.where(visible[None], scores, -1e30)
    top = jnp.max(scores, axis=-1, keepdims=True)
    expo = jnp.exp(scores - top)
    prob = expo / jnp.sum(expo, axis=-1, keepdims=True)
    prob_b = prob.astype(jnp.bfloat16)
    attn_out = jnp.einsum("hts,sd->thd", prob_b, values_all, preferred_element_type=jnp.float32)
    attn_out = attn_out.astype(jnp.bfloat16).reshape(tok_att, per_kv * head_dim)
    per_head = wide_n // heads_n
    own_rows = lax.dynamic_slice_in_dim(grad_resid, wide_at % per_head * tok_att, tok_att, 0)
    stacked = lax.all_gather(own_rows, "head", axis=0, tiled=True)
    resid_att = lax.dynamic_slice_in_dim(stacked, wide_at // per_head * tok_att, tok_att, 0)
    feature_cols = resid_att
    grad_heads_f = jnp.dot(
        feature_cols,
        lax.all_gather(out_proj, "wide", axis=0, tiled=True),
        preferred_element_type=jnp.float32,
    )
    feature_cols = resid_att
    grad_proj = lax.psum_scatter(
        lax.dot_general(
            feature_cols, attn_out, contract_first, preferred_element_type=jnp.float32
        ).astype(jnp.bfloat16),
        "wide",
        scatter_dimension=0,
        tiled=True,
    )
    grad_heads = grad_heads_f.astype(jnp.bfloat16).reshape(tok_att, per_kv, head_dim)
    dprob = jnp.einsum("thd,sd->hts", grad_heads, values_all, preferred_element_type=jnp.float32)
    delta = jnp.sum(prob * dprob, axis=-1, keepdims=True)
    dscore = (prob * (dprob - delta) * score_scale).astype(jnp.bfloat16)
    grad_query = jnp.einsum("hts,sd->thd", dscore, keys_all, preferred_element_type=jnp.float32)
    grad_query = grad_query.astype(jnp.bfloat16).reshape(tok_att, per_kv * head_dim)
    key_part = jnp.einsum("hts,thd->sd", dscore, query3, preferred_element_type=jnp.float32)
    value_part = jnp.einsum("hts,thd->sd", prob_b, grad_heads, preferred_element_type=jnp.float32)
    key_sum, value_sum = (
        lax.psum_scatter(
            key_part.astype(jnp.bfloat16), "wide", scatter_dimension=0, tiled=True
        ).astype(jnp.float32),
        lax.psum_scatter(
            value_part.astype(jnp.bfloat16), "wide", scatter_dimension=0, tiled=True
        ).astype(jnp.float32),
    )
    return (
        grad_resid,
        grad_gain,
        grad_gate,
        grad_up,
        grad_proj,
        grad_query,
        key_sum.astype(jnp.bfloat16),
        value_sum.astype(jnp.bfloat16),
    )


def solution(mesh):
    return jax.shard_map(
        local,
        mesh=mesh,
        in_specs=(
            P("head", None),
            P(),
            P(None, "wide"),
            P(None, "wide"),
            P("head", "wide"),
            P("head", None),
            P("wide", "head"),
            P("wide", "head"),
            P("wide", "head"),
            P("wide", "head"),
            P(),
        ),
        out_specs=(
            P("head", None),
            P(),
            P("head", "wide"),
            P("head", "wide"),
            P("wide", "head"),
            P("wide", "head"),
            P("wide", "head"),
            P("wide", "head"),
        ),
        check_vma=False,
    )
```

profile of v0, /device:TPU:8, one launch (start us, length us, event | category | flops | bytes accessed | tf_op | source)
XLA Modules:
  0.0 636.3 jit_solution(16114775944460666054)
XLA Ops:
  7.2 0.0 all-reduce.2.cloned.1.call-start
  7.2 2.2 fusion.12
  9.5 6.4 %fusion.37 = (bf16[256,896]{1,0:T(8,128)(2,1)S(1)}, f32[256,896]{1,0:T(8,128)S(1)}) fusion(bf16[256,896]{1,0:T(8,128)(2,1)} %param.15, bf16[4096,896]{1,0:T(8,128)(2,1)} %param.13, bf16[256,4096]{1,0:T(8,128)(2,1)} %param.11, f32[4096]{0:T(1024)} %param.12, f32[256]{0:T(256)S(1)} %add_rsqrt_fusion), kind=kOutput, calls=%fused_computation.54 | convolution fusion | flops 1884848128 | bytes 11289600 | tf_op jit(solution)/shard_map/dot_general | solution.py:34
  16.0 2.5 fusion.26
  18.6 2.4 fusion.92
  21.0 3.8 fusion.5
  24.8 0.0 all-reduce.2.cloned.1.call-update
  24.9 0.2 all-gather.3.cloned.1.call-start
  25.1 62.5 %all-reduce.2.cloned.1.call-done = bf16[256,4096]{1,0:T(8,128)(2,1)} async-done(((bf16[256,4096]{1,0:T(8,128)(2,1)}), bf16[256,4096]{1,0:T(8,128)(2,1)}) %all-reduce.2.cloned.1.call-update) | async-done | bytes 2097168 | tf_op jit(solution)/shard_map/psum | solution.py:46
  87.7 3.4 fusion.13
  91.1 1.7 fusion.9
  92.8 1.3 copy-done.3
  94.1 1.1 constant_dynamic-slice_fusion
  95.2 0.0 all-gather.3.cloned.1.call-update
  95.2 0.0 all-gather.5.cloned.1.call-start
  95.3 0.7 all-gather.5.cloned.1.call-update
  95.9 0.0 reduce-scatter.5.cloned.1.call-start
  96.0 7.7 %convolution_convert_fusion = bf16[4096,1792]{1,0:T(8,128)(2,1)} fusion(bf16[256,896]{1,0:T(8,128)(2,1)S(1)} %get-tuple-element.20, bf16[256,896]{1,0:T(8,128)(2,1)S(1)} %fusion.26, bf16[256,4096]{1,0:T(8,128)(2,1)S(1)} %copy-done.1, f32[4096]{0:T(1024)S(1)} %copy-done.5, f32[256]{0:T(256)S(1)} %add_rsqrt_fusion), kind=kOutput, calls=%fused_computation.2 | convolution fusion | flops 3771465728 | bytes 17712128 | tf_op jit(solution)/shard_map/dot_general | solution.py:49
  103.7 0.0 reduce-scatter.5.cloned.1.call-update
  103.7 0.0 reduce-scatter.11.cloned.1.call-start
  103.8 0.7 copy-done.7
  104.5 0.1 copy.20
  104.6 0.1 dynamic_slice.11
  104.7 8.4 %all_gather.14 = bf16[1024,128]{0,1:T(8,128)(2,1)S(1)} all-gather(bf16[128,128]{0,1:T(8,128)(2,1)S(1)} %copy.20), channel_id=1, replica_groups=mesh['head'=4,'wide'=8] {'wide'}, dimensions={0}, use_global_device_ids=true | all-gather | bytes 294912 | tf_op jit(solution)/shard_map/all_gather | solution.py:69
  113.0 9.3 %all_gather.13 = bf16[1024,128]{1,0:T(8,128)(2,1)S(1)} all-gather(bf16[128,128]{1,0:T(8,128)(2,1)S(1)} %copy-done.6), channel_id=1, replica_groups=mesh['head'=4,'wide'=8] {'wide'}, dimensions={0}, use_global_device_ids=true | all-gather | bytes 294912 | tf_op jit(solution)/shard_map/all_gather | solution.py:68
  122.3 0.2 fusion.41
  122.5 3.5 fusion.83
  126.0 2.7 convolution_convert_fusion.2
  128.7 44.0 %all-gather.3.cloned.1.call-done = bf16[512,4096]{1,0:T(8,128)(2,1)} async-done(((bf16[128,4096]{1,0:T(8,128)(2,1)}), bf16[512,4096]{1,0:T(8,128)(2,1)}) %all-gather.3.cloned.1.call-update) | async-done | bytes 4194320 | tf_op jit(solution)/shard_map/all_gather | solution.py:92
  172.7 57.5 %all-gather.5.cloned.1.call-done = bf16[4096,1024]{1,0:T(8,128)(2,1)} async-done(((bf16[512,1024]{1,0:T(8,128)(2,1)}), bf16[4096,1024]{1,0:T(8,128)(2,1)}) %all-gather.5.cloned.1.call-update) | async-done | bytes 8388624 | tf_op jit(solution)/shard_map/all_gather | solution.py:97
  230.2 5.1 fusion.31
  235.3 1.4 fusion.28
  236.7 0.0 reduce-scatter.11.cloned.1.call-update
  236.7 0.3 reduce-scatter.9.cloned.1.call-start
  237.0 3.4 fusion.45
  240.4 7.8 %fusion.29 = bf16[1024,128]{1,0:T(8,128)(2,1)} fusion(f32[128,8,1024]{0,2,1:T(8,128)} %fusion.45, f32[8,128,1024]{1,2,0:T(8,128)} %get-tuple-element.23, f32[8,128]{1,0:T(8,128)S(1)} %get-tuple-element.22, bf16[128,1024]{1,0:T(8,128)(2,1)S(1)} %copy-done), kind=kOutput, calls=%fused_computation.43 | convolution fusion | flops 275908608 | bytes 8916992 | tf_op jit(solution)/shard_map/hts,thd->sd/dot_general | solution.py:115
  248.2 0.0 reduce-scatter.9.cloned.1.call-update
  248.3 0.0 reduce-scatter.7.cloned.1.call-start
  248.3 6.9 %convolution_convert_fusion.1 = bf16[4096,1024]{1,0:T(8,128)(2,1)} fusion(bf16[128,1024]{0,1:T(8,128)(2,1)S(1)} %bitcast.120, bf16[512,4096]{1,0:T(8,128)(2,1)} %all-gather.3.cloned.1.call-done, s32[]{:T(128)S(6)} %select_n.27), kind=kOutput, calls=%fused_computation.3 | convolution fusion | flops 1077936128 | bytes 9699332 | tf_op jit(solution)/shard_map/dot_general | solution.py:102
  255.2 0.0 reduce-scatter.7.cloned.1.call-update
  255.2 16.1 %psum.15 = f32[4096]{0:T(1024)} all-reduce(f32[4096]{0:T(1024)S(1)} %get-tuple-element.16), channel_id=1, replica_groups=mesh['head'=4,'wide'=8] {'head'}, use_global_device_ids=true, to_apply=%region_4.0 | all-reduce | flops 4096 | bytes 32768 | tf_op jit(solution)/shard_map/psum | solution.py:58
  271.3 7.3 %fusion.30 = bf16[8,128,128]{1,2,0:T(8,128)(2,1)S(1)} fusion(f32[128,8,1024]{0,2,1:T(8,128)} %fusion.45, bf16[1024,128]{1,0:T(8,128)(2,1)S(1)} %all_gather.13, f32[8,128,1024]{1,2,0:T(8,128)} %get-tuple-element.23, f32[8,128]{1,0:T(8,128)S(1)} %get-tuple-element.22), kind=kOutput, calls=%fused_computation.44 | convolution fusion | flops 275908608 | bytes 8916992 | tf_op jit(solution)/shard_map/hts,sd->thd/dot_general | solution.py:113
  278.6 0.9 copy.29
  279.5 199.2 %reduce-scatter.5.cloned.1.call-done = bf16[1024,1792]{1,0:T(8,128)(2,1)} async-done(((bf16[4096,1792]{1,0:T(8,128)(2,1)}), bf16[1024,1792]{1,0:T(8,128)(2,1)}) %reduce-scatter.5.cloned.1.call-update) | async-done | bytes 3670032 | tf_op jit(solution)/shard_map/reduce_scatter | solution.py:48
  478.6 4.2 fusion.82
  482.8 34.0 %reduce-scatter.11.cloned.1.call-done = bf16[128,128]{1,0:T(8,128)(2,1)} async-done(((bf16[1024,128]{1,0:T(8,128)(2,1)}), bf16[128,128]{1,0:T(8,128)(2,1)}) %reduce-scatter.11.cloned.1.call-update) | async-done | bytes 32784 | tf_op jit(solution)/shard_map/reduce_scatter | solution.py:121
  516.8 37.4 %reduce-scatter.9.cloned.1.call-done = bf16[128,128]{1,0:T(8,128)(2,1)} async-done(((bf16[1024,128]{1,0:T(8,128)(2,1)}), bf16[128,128]{1,0:T(8,128)(2,1)}) %reduce-scatter.9.cloned.1.call-update) | async-done | bytes 32784 | tf_op jit(solution)/shard_map/reduce_scatter | solution.py:118
  554.1 75.3 %reduce-scatter.7.cloned.1.call-done = bf16[512,1024]{1,0:T(8,128)(2,1)} async-done(((bf16[4096,1024]{1,0:T(8,128)(2,1)}), bf16[512,1024]{1,0:T(8,128)(2,1)}) %reduce-scatter.7.cloned.1.call-update) | async-done | bytes 1048592 | tf_op jit(solution)/shard_map/reduce_scatter | solution.py:101
  (33 shorter events, 0.1 us)
Async XLA Ops:
  7.2 115.4 %copy-start = (bf16[128,1024]{1,0:T(8,128)(2,1)S(1)}, bf16[128,1024]{1,0:T(8,128)(2,1)}, u32[]{:S(2)}) copy-start(bf16[128,1024]{1,0:T(8,128)(2,1)} %param.18) | copy-start | bytes 786436
  7.2 80.5 %all-reduce.2.cloned.1.call-start = ((), (), s32[]{:S(2)}) async-start(), calls=%async_computation.4 | async-start | bytes 4194304 | tf_op jit(solution)/shard_map/psum | solution.py:46
  7.2 8.7 %slice-start = ((s8[7340032]{0:T(1024)(128)(4,1)}), s8[4194304]{0:T(1024)(128)(4,1)S(1)}, s32[]{:S(2)}) async-start(s8[7340032]{0:T(1024)(128)(4,1)} %bitcast.118), calls=%async_computation.11 | async-start | bytes 8388608
  9.5 6.5 %copy-start.1 = (bf16[256,4096]{1,0:T(8,128)(2,1)S(1)}, bf16[256,4096]{1,0:T(8,128)(2,1)}, u32[]{:S(2)}) copy-start(bf16[256,4096]{1,0:T(8,128)(2,1)} %param.11) | copy-start | bytes 6291460
  9.5 6.5 %slice-start.1 = ((s8[7340032]{0:T(1024)(128)(4,1)}), s8[3145728]{0:T(1024)(128)(4,1)S(1)}, s32[]{:S(2)}) async-start(s8[7340032]{0:T(1024)(128)(4,1)} %bitcast.118), calls=%async_computation.12 | async-start | bytes 6291456
  9.5 6.5 %copy-start.5 = (f32[4096]{0:T(1024)S(1)}, f32[4096]{0:T(1024)}, u32[]{:S(2)}) copy-start(f32[4096]{0:T(1024)} %param.12) | copy-start | bytes 49156
  9.5 6.5 %copy-start.9 = (bf16[256,896]{1,0:T(8,128)(2,1)S(1)}, bf16[256,896]{1,0:T(8,128)(2,1)}, u32[]{:S(2)}) copy-start(bf16[256,896]{1,0:T(8,128)(2,1)} %param.15) | copy-start | bytes 1376260
  9.5 9.0 %slice-start.2 = ((s8[7340032]{0:T(1024)(128)(4,1)}), s8[4194304]{0:T(1024)(128)(4,1)S(1)}, s32[]{:S(2)}) async-start(s8[7340032]{0:T(1024)(128)(4,1)} %bitcast.122), calls=%async_computation.13 | async-start | bytes 8388608
  15.9 2.6 slice-start.3
  24.9 147.8 %all-gather.3.cloned.1.call-start = ((), (), s32[]{:S(2)}) async-start(), calls=%async_computation.6 | async-start | bytes 5242880 | tf_op jit(solution)/shard_map/all_gather | solution.py:92
  87.7 3.4 copy-start.2
  87.7 3.4 copy-start.4
  92.8 1.3 copy-start.3
  95.2 134.9 %all-gather.5.cloned.1.call-start = ((), (), s32[]{:S(2)}) async-start(), calls=%async_computation.8 | async-start | bytes 9437184 | tf_op jit(solution)/shard_map/all_gather | solution.py:97
  95.9 382.7 %reduce-scatter.5.cloned.1.call-start = ((), (), s32[]{:S(2)}) async-start(), calls=%async_computation.5 | async-start | bytes 18350080 | tf_op jit(solution)/shard_map/reduce_scatter | solution.py:48
  103.7 0.8 copy-start.7
  103.7 0.9 copy-start.8
  103.7 9.3 %copy-start.6 = (bf16[128,128]{1,0:T(8,128)(2,1)S(1)}, bf16[128,128]{1,0:T(8,128)(2,1)}, u32[]{:S(2)}) copy-start(bf16[128,128]{1,0:T(8,128)(2,1)} %param.19) | copy-start | bytes 98308
  103.7 413.0 %reduce-scatter.11.cloned.1.call-start = ((), (), s32[]{:S(2)}) async-start(), calls=%async_computation.10 | async-start | bytes 294912 | tf_op jit(solution)/shard_map/reduce_scatter | solution.py:121
  230.2 5.1 copy-start.10
  236.7 317.4 %reduce-scatter.9.cloned.1.call-start = ((), (), s32[]{:S(2)}) async-start(), calls=%async_computation.9 | async-start | bytes 294912 | tf_op jit(solution)/shard_map/reduce_scatter | solution.py:118
  248.3 381.2 %reduce-scatter.7.cloned.1.call-start = ((), (), s32[]{:S(2)}) async-start(), calls=%async_computation.7 | async-start | bytes 9437184 | tf_op jit(solution)/shard_map/reduce_scatter | solution.py:101
Sparse Core Ops, SparseCore 0:
  25.0 62.6 all-reduce.1
  95.3 77.2 all-gather.2
  174.6 55.5 all-gather.4
  232.4 246.2 reduce-scatter.4
  482.1 34.6 reduce-scatter.10
  520.5 33.5 reduce-scatter.8
  558.2 71.2 reduce-scatter.6
where the time goes:
time: 638 us; the launch traced here: 636 us
  waiting for transfers between devices  511 us (80%)
  matrix products  61 us (10%)
  blocking collectives  33.8 us (5%)
  between operations  14.4 us (2%)
  local copies, waits for them, and re-layouts  8.33 us (1%)
  other arithmetic  7.57 us (1%)
    reduce_scatter x1, waiting for transfers between devices, local(): lax.psum_scatter(lax.dot_general(normed, both_grads, contract_first, pref...  199 us
    reduce_scatter x1, waiting for transfers between devices, local(): lax.psum_scatter(lax.dot_general(feature_cols, attn_out, contract_first,...  75.3 us
    psum x1, waiting for transfers between devices, local(): lax.psum(partial_norm.astype(jnp.bfloat16), 'wide').astype(jnp.float32)  62.5 us
    all_gather x1, waiting for transfers between devices, local(): lax.all_gather(out_proj, 'wide', axis=0, tiled=True)  57.5 us
    all_gather x1, waiting for transfers between devices, local(): stacked = lax.all_gather(own_rows, 'head', axis=0, tiled=True)  44 us
    reduce_scatter x1, waiting for transfers between devices, local(): lax.psum_scatter(key_part.astype(jnp.bfloat16), 'wide', scatter_dimension...  37.4 us
    reduce_scatter x1, waiting for transfers between devices, local(): lax.psum_scatter(value_part.astype(jnp.bfloat16), 'wide', scatter_dimensi...  34 us
    psum x1, blocking collectives, local(): grad_gain = lax.psum(jnp.sum(grad_norm * normed_f, axis=0), 'head')  16.1 us
  transfers between devices with their start and end apart: 7, of which 7 were waited for; matrix products, arithmetic and copies ran while one was open for 8% of the time, Pallas kernels for 0%

commit v1 on v0

v1 whole, which is shorter than its diff:
```python
import functools
import math

import jax
import jax.numpy as jnp
from jax import lax
from jax.experimental import pallas as pl
from jax.experimental.pallas import tpu as pltpu
from jax.sharding import PartitionSpec as P

EPSILON = 1e-05
MESH = pl.DeviceIdType.MESH
ANY = pl.BlockSpec(memory_space=pl.ANY)
VMEM = pl.BlockSpec(memory_space=pltpu.VMEM)


def enter(groups):
    barrier = pltpu.get_barrier_semaphore()
    total = 0
    for axis, n in groups:
        me = lax.axis_index(axis)
        for k in range(1, n):
            pl.semaphore_signal(
                barrier, inc=1, device_id={axis: lax.rem(me + k, n)}, device_id_type=MESH
            )
        total += n - 1
    pl.semaphore_wait(barrier, total)


def part(ref, dim, index, size):
    start = pl.multiple_of(index * size, size)
    if dim == 0:
        return ref.at[pl.ds(start, size)]
    return ref.at[:, pl.ds(start, size)]


def params(collective_id):
    return pltpu.CompilerParams(
        collective_id=collective_id, has_side_effects=True, vmem_limit_bytes=32 * 1024 * 1024
    )


def scatter_sum_kernel(axis, n, dim, src, out, held, send_sem, recv_sem, own_sem):
    me = lax.axis_index(axis)
    size = out.shape[dim]
    own = pltpu.make_async_copy(part(src, dim, me, size), held.at[0], own_sem)
    own.start()
    enter([(axis, n)])
    copies = []
    for k in range(1, n):
        peer = lax.rem(me + k, n)
        copies.append(
            pltpu.make_async_remote_copy(
                src_ref=part(src, dim, peer, size),
                dst_ref=held.at[k],
                send_sem=send_sem.at[k],
                recv_sem=recv_sem.at[k],
                device_id={axis: peer},
                device_id_type=MESH,
            )
        )
        copies[-1].start()
    own.wait()
    for copy in copies:
        copy.wait()
    step = 32

    @pl.loop(0, out.shape[0] // step)
    def _(i):
        rows = pl.ds(pl.multiple_of(i * step, step), step)
        total = held[0, rows].astype(jnp.float32)
        for k in range(1, n):
            total = total + held[k, rows].astype(jnp.float32)
        out[rows] = total.astype(out.dtype)


def scatter_sum(x, axis, dim, collective_id):
    n = lax.axis_size(axis)
    shape = list(x.shape)
    shape[dim] //= n
    return pl.pallas_call(
        functools.partial(scatter_sum_kernel, axis, n, dim),
        out_shape=jax.ShapeDtypeStruct(tuple(shape), x.dtype),
        in_specs=[ANY],
        out_specs=VMEM,
        scratch_shapes=[
            pltpu.VMEM((n, *shape), x.dtype),
            pltpu.SemaphoreType.DMA((n,)),
            pltpu.SemaphoreType.DMA((n,)),
            pltpu.SemaphoreType.DMA,
        ],
        compiler_params=params(collective_id),
    )(x)


def gather_kernel(plan, *refs):
    count = len(plan)
    srcs, outs = refs[:count], refs[count : 2 * count]
    sems = refs[2 * count :]
    groups = []
    for axis, n, _ in plan:
        if (axis, n) not in groups:
            groups.append((axis, n))
    owns = []
    for i, (axis, n, dim) in enumerate(plan):
        me = lax.axis_index(axis)
        own = pltpu.make_async_copy(
            srcs[i], part(outs[i], dim, me, srcs[i].shape[dim]), sems[3 * i + 2]
        )
        own.start()
        owns.append(own)
    enter(groups)
    copies = []
    for i, (axis, n, dim) in enumerate(plan):
        me = lax.axis_index(axis)
        for k in range(1, n):
            copy = pltpu.make_async_remote_copy(
                src_ref=srcs[i],
                dst_ref=part(outs[i], dim, me, srcs[i].shape[dim]),
                send_sem=sems[3 * i].at[k],
                recv_sem=sems[3 * i + 1].at[k],
                device_id={axis: lax.rem(me + k, n)},
                device_id_type=MESH,
            )
            copy.start()
            copies.append(copy)
    for own in owns:
        own.wait()
    for copy in copies:
        copy.wait()


def gather(arrays, axes_dims, collective_id):
    plan, outs, scratch = [], [], []
    for x, (axis, dim) in zip(arrays, axes_dims):
        n = lax.axis_size(axis)
        plan.append((axis, n, dim))
        shape = list(x.shape)
        shape[dim] *= n
        outs.append(jax.ShapeDtypeStruct(tuple(shape), x.dtype))
        scratch += [
            pltpu.SemaphoreType.DMA((n,)),
            pltpu.SemaphoreType.DMA((n,)),
            pltpu.SemaphoreType.DMA,
        ]
    return pl.pallas_call(
        functools.partial(gather_kernel, plan),
        out_shape=outs,
        in_specs=[ANY] * len(arrays),
        out_specs=[ANY] * len(arrays),
        scratch_shapes=scratch,
        compiler_params=params(collective_id),
    )(*arrays)


def shifted(x, axis, n, k):
    return lax.ppermute(x, axis, [(i, (i + k) % n) for i in range(n)])


def local(
    residual,
    norm_gain,
    w_gate,
    w_up,
    grad_hidden,
    grad_out,
    out_proj,
    queries,
    keys_in,
    values_in,
    doc_ids,
):
    heads_n = lax.axis_size("head")
    wide_n = lax.axis_size("wide")
    head_at = lax.axis_index("head")
    wide_at = lax.axis_index("wide")
    tok_mlp, width = residual.shape
    cols_wide = width // wide_n
    cols_head = width // heads_n
    contract_last = (((1,), (1,)), ((), ()))
    contract_first = (((0,), (0,)), ((), ()))
    tok_att = queries.shape[0]
    head_dim = keys_in.shape[1]
    per_kv = queries.shape[1] // head_dim
    score_scale = 1.0 / math.sqrt(head_dim)

    kv_all = lax.all_gather(
        jnp.concatenate([keys_in, values_in], axis=1), "wide", axis=0, tiled=True
    )
    keys_all, values_all = kv_all[:, :head_dim], kv_all[:, head_dim:]

    resid_f = residual.astype(jnp.float32)
    inv_rms = lax.rsqrt(jnp.mean(resid_f * resid_f, axis=-1, keepdims=True) + EPSILON)
    normed = (resid_f * inv_rms * norm_gain).astype(jnp.bfloat16)

    def normed_cols(owner):
        return lax.dynamic_slice_in_dim(normed, owner * cols_head, cols_head, 1)

    normed_parts = [normed_cols(head_at)]
    for k in range(1, heads_n):
        normed_parts.append(
            shifted(normed_cols(lax.rem(head_at + k, heads_n)), "head", heads_n, k)
        )

    gate_pre = jnp.dot(normed, w_gate, preferred_element_type=jnp.float32)
    up_pre = jnp.dot(normed, w_up, preferred_element_type=jnp.float32)
    sigma = jax.nn.sigmoid(gate_pre)
    grad_h = grad_hidden.astype(jnp.float32)
    grad_g = (grad_h * up_pre * sigma * (1.0 + gate_pre * (1.0 - sigma))).astype(jnp.bfloat16)
    grad_u = (grad_h * gate_pre * sigma).astype(jnp.bfloat16)
    partial_norm = lax.dot_general(
        grad_g, w_gate, contract_last, preferred_element_type=jnp.float32
    )
    partial_norm = partial_norm + lax.dot_general(
        grad_u, w_up, contract_last, preferred_element_type=jnp.float32
    )
    gate_parts, up_parts = [grad_g], [grad_u]
    for k in range(1, heads_n):
        gate_parts.append(shifted(grad_g, "head", heads_n, k))
        up_parts.append(shifted(grad_u, "head", heads_n, k))

    grad_norm = scatter_sum(partial_norm.astype(jnp.bfloat16), "wide", 1, 1).astype(jnp.float32)
    resid_own = lax.dynamic_slice_in_dim(residual, wide_at * cols_wide, cols_wide, 1)
    normed_own = resid_own.astype(jnp.float32) * inv_rms
    gain_own = lax.dynamic_slice_in_dim(norm_gain, wide_at * cols_wide, cols_wide, 0)
    out_own = lax.dynamic_slice_in_dim(grad_out, wide_at * cols_wide, cols_wide, 1)
    product = grad_norm * normed_own
    stats = jnp.concatenate([jnp.sum(product * gain_own, axis=1), jnp.sum(product, axis=0)])
    stat_len = -(-stats.shape[0] // 1024) * 1024
    stats = jnp.pad(stats, (0, stat_len - stats.shape[0])).reshape(stat_len // 128, 128)
    (stats_all,) = gather([stats], [("wide", 0)], 2)
    stats_all = stats_all.reshape(wide_n, stat_len)
    mean_term = (jnp.sum(stats_all[:, :tok_mlp], axis=0) / width)[:, None]
    gain_part = stats_all[:, tok_mlp : tok_mlp + cols_wide].reshape(width // 128, 128)
    resid_grad = (
        out_own.astype(jnp.float32) + inv_rms * (grad_norm * gain_own - normed_own * mean_term)
    ).astype(jnp.bfloat16)
    resid_cols, gain_all = gather([resid_grad, gain_part], [("head", 0), ("head", 0)], 3)
    grad_gain = jnp.sum(gain_all.reshape(heads_n, width), axis=0)
    grad_resid = lax.all_gather(resid_grad, "wide", axis=1, tiled=True)

    tok_total = keys_all.shape[0]
    q_offset = wide_at * tok_att
    positions = jnp.arange(tok_total, dtype=jnp.int32)
    q_pos = q_offset + jnp.arange(tok_att, dtype=jnp.int32)
    q_docs = lax.dynamic_slice_in_dim(doc_ids, q_offset, tok_att, 0)
    visible = (q_docs[:, None] == doc_ids[None, :]) & (positions[None, :] <= q_pos[:, None])
    query3 = queries.reshape(tok_att, per_kv, head_dim)
    scores = (
        jnp.einsum("thd,sd->hts", query3, keys_all, preferred_element_type=jnp.float32)
        * score_scale
    )
    scores = jnp.where(visible[None], scores, -1e30)
    top = jnp.max(scores, axis=-1, keepdims=True)
    expo = jnp.exp(scores - top)
    prob = expo / jnp.sum(expo, axis=-1, keepdims=True)
    prob_b = prob.astype(jnp.bfloat16)
    attn_out = jnp.einsum("hts,sd->thd", prob_b, values_all, preferred_element_type=jnp.float32)
    attn_out = attn_out.astype(jnp.bfloat16).reshape(tok_att, per_kv * head_dim)
    attn_all = lax.all_gather(attn_out, "wide", axis=0, tiled=True)

    heads_part = jnp.dot(resid_cols, out_proj, preferred_element_type=jnp.float32)
    grad_heads = scatter_sum(heads_part.astype(jnp.bfloat16), "wide", 0, 4)
    grad_heads = grad_heads.reshape(tok_att, per_kv, head_dim)
    dprob = jnp.einsum("thd,sd->hts", grad_heads, values_all, preferred_element_type=jnp.float32)
    delta = jnp.sum(prob * dprob, axis=-1, keepdims=True)
    dscore = (prob * (dprob - delta) * score_scale).astype(jnp.bfloat16)
    grad_query = jnp.einsum("hts,sd->thd", dscore, keys_all, preferred_element_type=jnp.float32)
    grad_query = grad_query.astype(jnp.bfloat16).reshape(tok_att, per_kv * head_dim)
    key_part = jnp.einsum("hts,thd->sd", dscore, query3, preferred_element_type=jnp.float32)
    value_part = jnp.einsum("hts,thd->sd", prob_b, grad_heads, preferred_element_type=jnp.float32)
    kv_sum = scatter_sum(
        jnp.concatenate([key_part, value_part], axis=1).astype(jnp.bfloat16), "wide", 0, 5
    )

    grad_proj = lax.dot_general(
        resid_cols, attn_all, contract_first, preferred_element_type=jnp.float32
    ).astype(jnp.bfloat16)
    normed_all = jnp.concatenate(normed_parts, axis=0)
    grad_gate = lax.dot_general(
        normed_all,
        jnp.concatenate(gate_parts, axis=0),
        contract_first,
        preferred_element_type=jnp.float32,
    ).astype(jnp.bfloat16)
    grad_up = lax.dot_general(
        normed_all,
        jnp.concatenate(up_parts, axis=0),
        contract_first,
        preferred_element_type=jnp.float32,
    ).astype(jnp.bfloat16)
    return (
        grad_resid,
        grad_gain,
        grad_gate,
        grad_up,
        grad_proj,
        grad_query,
        kv_sum[:, :head_dim],
        kv_sum[:, head_dim:],
    )


def solution(mesh):
    return jax.shard_map(
        local,
        mesh=mesh,
        in_specs=(
            P("head", None),
            P(),
            P(None, "wide"),
            P(None, "wide"),
            P("head", "wide"),
            P("head", None),
            P("wide", "head"),
            P("wide", "head"),
            P("wide", "head"),
            P("wide", "head"),
            P(),
        ),
        out_specs=(
            P("head", None),
            P(),
            P("head", "wide"),
            P("head", "wide"),
            P("wide", "head"),
            P("wide", "head"),
            P("wide", "head"),
            P("wide", "head"),
        ),
        check_vma=False,
    )
```

time: 638 us -> 288 us (0.45)
  waiting for transfers between devices: 511 us -> 34.7 us
  Pallas kernels: 0 us -> 137 us
  blocking collectives: 33.8 us -> 9.86 us
  starting transfers between devices: 0.69 us -> 12.9 us
    reduce_scatter x4 -> x0, waiting for transfers between devices: 346 us -> none  [the longest x1 199 us: local(): lax.psum_scatter(lax.dot_general(normed, both_grads, contract_first, pref...]
    pallas_call x0 -> x5, Pallas kernels: none -> 137 us  [the longest x2 74.6 us: gather(): pl.pallas_call(functools.partial(gather_kernel, plan), out_shape=outs, in...]
    all_gather x2, waiting for transfers between devices: 101 us -> 0.01 us  [the longest x1 0.01 us: local(): attn_all = lax.all_gather(attn_out, 'wide', axis=0, tiled=True)]
    psum x1 -> x0, waiting for transfers between devices: 62.5 us -> none  [local(): lax.psum(partial_norm.astype(jnp.bfloat16), 'wide').astype(jnp.float32)]
    ppermute x0 -> x9, waiting for transfers between devices: none -> 34.7 us  [shifted(): return lax.ppermute(x, axis, [(i, (i + k) % n) for i in range(n)])]
    psum x1 -> x0, blocking collectives: 16.1 us -> none  [local(): grad_gain = lax.psum(jnp.sum(grad_norm * normed_f, axis=0), 'head')]
    ppermute x0 -> x9, starting transfers between devices: none -> 12.8 us  [shifted(): return lax.ppermute(x, axis, [(i, (i + k) % n) for i in range(n)])]
    all_gather x2 -> x1, blocking collectives: 17.7 us -> 9.86 us  [local(): lax.all_gather(jnp.concatenate([keys_in, values_in], axis=1), 'wide', axi...]
  transfers between devices with their start and end apart: 7 -> 11, of which waited for: 7 -> 4; matrix products, arithmetic and copies ran while one was open for 8% -> 22% of each run, Pallas kernels for 0% -> 48%
where the time goes in v1:
time: 288 us; the launch traced here: 287 us
  Pallas kernels  137 us (48%)
  matrix products  60.5 us (21%)
  waiting for transfers between devices  34.7 us (12%)
  between operations  14.4 us (5%)
  starting transfers between devices  12.9 us (4%)
  local copies, waits for them, and re-layouts  10.9 us (4%)
  blocking collectives  9.86 us (3%)
  other arithmetic  6.72 us (2%)
    pallas_call x2, Pallas kernels, gather(): pl.pallas_call(functools.partial(gather_kernel, plan), out_shape=outs, in...  74.6 us
    pallas_call x3, Pallas kernels, scatter_sum(): pl.pallas_call(functools.partial(scatter_sum_kernel, axis, n, dim), out_s...  62.6 us
    ppermute x9, waiting for transfers between devices, shifted(): return lax.ppermute(x, axis, [(i, (i + k) % n) for i in range(n)])  34.7 us
    ppermute x9, starting transfers between devices, shifted(): return lax.ppermute(x, axis, [(i, (i + k) % n) for i in range(n)])  12.8 us
    all_gather x1, blocking collectives, local(): lax.all_gather(jnp.concatenate([keys_in, values_in], axis=1), 'wide', axi...  9.86 us
    dot_general x1, matrix products, local(): jnp.einsum('hts,sd->thd', dscore, keys_all, preferred_element_type=jnp.fl...  7.91 us
    dot_general x1, matrix products, local(): jnp.einsum('hts,thd->sd', dscore, query3, preferred_element_type=jnp.floa...  7.83 us
    dot_general x1, matrix products, local(): gate_pre = jnp.dot(normed, w_gate, preferred_element_type=jnp.float32)  7.41 us
  transfers between devices with their start and end apart: 11, of which 4 were waited for; matrix products, arithmetic and copies ran while one was open for 22% of the time, Pallas kernels for 48%

profile of v1, /device:TPU:8, one launch (start us, length us, event | category | flops | bytes accessed | tf_op | source)
XLA Modules:
  0.0 287.1 jit_solution(7230476140194722247)
XLA Ops:
  7.2 0.9 pad_maximum_fusion.4
  8.1 9.9 %all_gather.10 = bf16[1024,256]{1,0:T(8,128)(2,1)S(1)} all-gather(bf16[128,256]{1,0:T(8,128)(2,1)S(1)} %pad_maximum_fusion.4), channel_id=1, replica_groups=mesh['head'=4,'wide'=8] {'wide'}, dimensions={0}, use_global_device_ids=true | all-gather | bytes 589824 | tf_op jit(solution)/shard_map/all_gather | solution.py:187
  18.0 1.3 copy.44
  19.3 0.8 dynamic_slice.31
  20.1 0.9 fusion.53
  20.9 3.4 %fusion.69 = (f32[8,128]{1,0:T(8,128)S(1)}, f32[8,128,1024]{1,2,0:T(8,128)}) fusion(pred[128,1024]{0,1:T(8,128)(4,1)S(1)} %fusion.53, bf16[128,8,128]{0,2,1:T(8,128)(2,1)S(1)} %bitcast.102, bf16[1024,256]{1,0:T(8,128)(2,1)S(1)} %all_gather.10), kind=kOutput, calls=%fused_computation.99 | convolution fusion | flops 272630784 | bytes 4853760 | tf_op jit(solution)/shard_map/sub | solution.py:255
  24.4 3.6 %convolution_convert_fusion.2 = bf16[128,8,128]{2,0,1:T(8,128)(2,1)} fusion(bf16[1024,256]{1,0:T(8,128)(2,1)} %copy-done.4, f32[8,128,1024]{1,2,0:T(8,128)} %get-tuple-element.31, f32[8,128]{1,0:T(8,128)S(1)} %get-tuple-element.30), kind=kOutput, calls=%fused_computation.54 | convolution fusion | flops 270663680 | bytes 4722688 | tf_op jit(solution)/shard_map/hts,sd->thd/dot_general | solution.py:258
  28.0 0.5 fusion.3
  28.6 0.6 fusion.5
  29.3 7.4 %fusion.48 = (bf16[256,896]{1,0:T(8,128)(2,1)}, f32[256,896]{1,0:T(8,128)S(1)}) fusion(bf16[256,896]{1,0:T(8,128)(2,1)S(1)} %copy-done.11, bf16[256,4096]{1,0:T(8,128)(2,1)S(1)} %fusion.5, bf16[4096,896]{1,0:T(8,128)(2,1)} %param.13), kind=kOutput, calls=%fused_computation.59 | convolution fusion | flops 1880653824 | bytes 11272192 | tf_op jit(solution)/shard_map/dot_general | solution.py:205
  36.7 1.6 collective-permute-start.6
  38.2 1.3 collective-permute-start.7
  39.5 2.4 fusion.40
  42.0 2.4 fusion.70
  44.4 3.5 %fusion.2.src = bf16[256,4096]{1,0:T(8,128)(2,1)S(1)} fusion(f32[256,4096]{1,0:T(8,128)S(1)} %fusion.70, bf16[256,896]{1,0:T(8,128)(2,1)} %get-tuple-element.28, bf16[4096,896]{1,0:T(8,128)(2,1)S(1)} %bitcast.98), kind=kOutput, calls=%fused_computation.5 | convolution fusion | flops 1881145344 | bytes 14090240 | tf_op jit(solution)/shard_map/dot_general | solution.py:214
  47.9 27.7 %shard_map.170 = bf16[256,512]{1,0:T(8,128)(2,1)S(1)} custom-call(bf16[256,4096]{1,0:T(8,128)(2,1)S(1)} %fusion.2.src), custom_call_target="tpu_custom_call" | custom-call | tf_op jit(solution)/shard_map/pallas_call | solution.py:81
  75.6 0.1 dynamic_slice.25
  75.7 0.3 multiply_reduce_fusion
  76.0 6.2 %shard_map.171 = f32[64,128]{1,0:T(8,128)S(1)} custom-call(f32[8,128]{1,0:T(8,128)S(1)} %fusion.59.refs_0_), custom_call_target="tpu_custom_call" | custom-call | tf_op jit(solution)/shard_map/pallas_call | solution.py:146
  82.2 1.9 fusion.52.refs_0_
  84.1 2.9 %constant_dynamic-slice_fusion.3 = (bf16[256,1024]{1,0:T(8,128)(2,1)}, bf16[256,1024]{1,0:T(8,128)(2,1)}, bf16[256,1024]{1,0:T(8,128)(2,1)}, bf16[256,1024]{1,0:T(8,128)(2,1)}) fusion(bf16[256,4096]{1,0:T(8,128)(2,1)} %copy-done.3, s32[]{:T(128)S(6)} %select_n.25, s32[]{:T(128)S(6)} %select_n.28, s32[]{:T(128)S(6)} %select_n.27, s32[]{:T(128)S(6)} %select_n.26), kind=kLoop, calls=%fused_computation.86 | loop fusion | bytes 4194320 | tf_op jit(solution)/shard_map/dynamic_slice | solution.py:197
  87.0 1.5 collective-permute-start
  88.5 1.4 collective-permute-start.1
  89.9 1.5 collective-permute-start.2
  91.5 68.4 %shard_map.172 = (bf16[1024,512]{1,0:T(8,128)(2,1)S(1)}, f32[128,128]{1,0:T(8,128)S(1)}) custom-call(bf16[256,512]{1,0:T(8,128)(2,1)S(1)} %copy-done.1, f32[32,128]{1,0:T(8,128)S(1)} %reshape.109.refs_1_), custom_call_target="tpu_custom_call" | custom-call | tf_op jit(solution)/shard_map/pallas_call | solution.py:146
  159.9 1.3 convolution_convert_fusion.src
  161.2 25.0 %shard_map.173 = bf16[128,1024]{1,0:T(8,128)(2,1)S(1)} custom-call(bf16[1024,1024]{1,0:T(8,128)(2,1)S(1)} %convolution_convert_fusion.src), custom_call_target="tpu_custom_call" | custom-call | tf_op jit(solution)/shard_map/pallas_call | solution.py:81
  186.1 0.2 copy.45
  186.3 3.7 %fusion.42 = bf16[1024,128]{1,0:T(8,128)(2,1)} fusion(bf16[128,8,128]{0,2,1:T(8,128)(2,1)S(1)} %bitcast.99, f32[8,128,1024]{1,2,0:T(8,128)} %get-tuple-element.31, f32[8,128]{1,0:T(8,128)S(1)} %get-tuple-element.30), kind=kOutput, calls=%fused_computation.51 | convolution fusion | flops 270663680 | bytes 4722688 | tf_op jit(solution)/shard_map/hts,thd->sd/dot_general | solution.py:271
  190.0 2.7 fusion.57
  192.7 7.8 %fusion.43 = bf16[1024,128]{1,0:T(8,128)(2,1)} fusion(bf16[128,8,128]{0,2,1:T(8,128)(2,1)S(1)} %bitcast.103, f32[1024,128,8]{1,0,2:T(8,128)} %fusion.57, f32[8,128,1024]{1,2,0:T(8,128)} %get-tuple-element.31, f32[8,128]{1,0:T(8,128)S(1)} %get-tuple-element.30), kind=kOutput, calls=%fused_computation.52 | convolution fusion | flops 275908608 | bytes 8916992 | tf_op jit(solution)/shard_map/hts,thd->sd/dot_general | solution.py:270
  200.5 1.0 pad_maximum_fusion.1.src
  201.5 9.9 %shard_map.174 = bf16[128,256]{1,0:T(8,128)(2,1)S(1)} custom-call(bf16[1024,256]{1,0:T(8,128)(2,1)S(1)} %pad_maximum_fusion.1.src), custom_call_target="tpu_custom_call" | custom-call | tf_op jit(solution)/shard_map/pallas_call | solution.py:81
  211.5 1.5 collective-permute-start.8
  213.0 7.9 %fusion.44 = bf16[128,8,128]{2,0,1:T(8,128)(2,1)} fusion(f32[1024,128,8]{1,0,2:T(8,128)} %fusion.57, bf16[1024,256]{1,0:T(8,128)(2,1)S(1)} %copy-done.5, f32[8,128,1024]{1,2,0:T(8,128)} %get-tuple-element.31, f32[8,128]{1,0:T(8,128)S(1)} %get-tuple-element.30), kind=kOutput, calls=%fused_computation.53 | convolution fusion | flops 275908608 | bytes 17309696 | tf_op jit(solution)/shard_map/hts,sd->thd/dot_general | solution.py:268
  220.9 1.8 copy.31
  222.7 0.6 reduce_sum.67
  223.3 0.6 fusion.68
  224.0 0.8 collective-permute-start.3
  224.8 0.6 collective-permute-done.8
  225.4 3.3 %collective-permute-start.4 = (bf16[256,896]{1,0:T(8,128)(2,1)}, bf16[256,896]{1,0:T(8,128)(2,1)S(1)}, u32[]{:S(2)}, u32[]{:S(2)}) collective-permute-start(bf16[256,896]{1,0:T(8,128)(2,1)} %copy-done.12), channel_id=1, source_target_pairs={{0,16},{8,24},{16,0},{24,8},{1,17},{9,25},{17,1},{25,9},{2,18},{10... | collective-permute-start | bytes 1376264 | tf_op jit(solution)/shard_map/ppermute | solution.py:157
  228.7 5.6 %fusion.32 = bf16[1024,896]{1,0:T(8,128)(2,1)} fusion(bf16[256,896]{1,0:T(8,128)(2,1)} %collective-permute-done.8, bf16[256,896]{1,0:T(8,128)(2,1)} %collective-permute-done.7, bf16[256,896]{1,0:T(8,128)(2,1)} %collective-permute-done.6, bf16[256,896]{1,0:T(8,128)(2,1)} %get-tuple-element.28, bf16[256,1024]{1,0:T(8,128)(2,1)} %collective-permute-done.2, ...), kind=kOutput, calls=%fused_computation.42 | convolution fusion | flops 1895694336 | bytes 5767168 | tf_op jit(solution)/shard_map/dot_general | solution.py:286
  234.2 3.3 %collective-permute-done.3 = bf16[256,896]{1,0:T(8,128)(2,1)S(1)} collective-permute-done((bf16[256,896]{1,0:T(8,128)(2,1)}, bf16[256,896]{1,0:T(8,128)(2,1)S(1)}, u32[]{:S(2)}, u32[]{:S(2)}) %collective-permute-start.3) | collective-permute-done | bytes 458784 | tf_op jit(solution)/shard_map/ppermute | solution.py:157
  237.6 27.7 %collective-permute-done.4 = bf16[256,896]{1,0:T(8,128)(2,1)S(1)} collective-permute-done((bf16[256,896]{1,0:T(8,128)(2,1)}, bf16[256,896]{1,0:T(8,128)(2,1)S(1)}, u32[]{:S(2)}, u32[]{:S(2)}) %collective-permute-start.4) | collective-permute-done | bytes 458784 | tf_op jit(solution)/shard_map/ppermute | solution.py:157
  265.3 3.0 %collective-permute-done.5 = bf16[256,896]{1,0:T(8,128)(2,1)S(1)} collective-permute-done((bf16[256,896]{1,0:T(8,128)(2,1)}, bf16[256,896]{1,0:T(8,128)(2,1)S(1)}, u32[]{:S(2)}, u32[]{:S(2)}) %collective-permute-start.5) | collective-permute-done | bytes 458784 | tf_op jit(solution)/shard_map/ppermute | solution.py:157
  268.3 5.0 %fusion.35 = bf16[1024,896]{1,0:T(8,128)(2,1)} fusion(bf16[256,896]{1,0:T(8,128)(2,1)S(1)} %collective-permute-done.5, bf16[256,896]{1,0:T(8,128)(2,1)S(1)} %collective-permute-done.4, bf16[256,896]{1,0:T(8,128)(2,1)S(1)} %collective-permute-done.3, bf16[256,896]{1,0:T(8,128)(2,1)S(1)} %copy-done.13, bf16[256,1024]{1,0:T(8,128)(2,1)} %collective-permute-done.2, ...), kind=kOutput, calls=%fused_computation.43 | convolution fusion | flops 1895694336 | bytes 5767168 | tf_op jit(solution)/shard_map/dot_general | solution.py:280
  273.3 3.9 %convolution_convert_fusion.1 = bf16[512,1024]{1,0:T(8,128)(2,1)} fusion(bf16[1024,512]{1,0:T(8,128)(2,1)S(1)} %get-tuple-element.11, bf16[1024,1024]{0,1:T(8,128)(2,1)} %all-gather.5.cloned.1.call-done), kind=kOutput, calls=%fused_computation.44 | convolution fusion | flops 1074266112 | bytes 4194304 | tf_op jit(solution)/shard_map/dot_general | solution.py:276
  277.2 3.1 %copy.47 = bf16[256,4096]{1,0:T(8,128)(2,1)} copy(bf16[256,4096]{1,0:T(8,128)(2,1)} %all-gather.3.cloned.1.call-done) | data formatting | bytes 4194304
  (59 shorter events, 0.3 us)
Async XLA Ops:
  7.2 152.7 %copy-start = (bf16[512,1024]{1,0:T(8,128)(2,1)S(1)}, bf16[512,1024]{1,0:T(8,128)(2,1)}, u32[]{:S(2)}) copy-start(bf16[512,1024]{1,0:T(8,128)(2,1)} %param.17) | copy-start | bytes 3145732
  7.2 266.1 %all-gather.5.cloned.1.call-start = ((), (), s32[]{:S(2)}) async-start(), calls=%async_computation.1 | async-start | bytes 2359296 | tf_op jit(solution)/shard_map/all_gather | solution.py:260
  18.0 6.4 %copy-start.4 = (bf16[1024,256]{1,0:T(8,128)(2,1)}, bf16[1024,256]{1,0:T(8,128)(2,1)S(1)}, u32[]{:S(2)}) copy-start(bf16[1024,256]{1,0:T(8,128)(2,1)S(1)} %all_gather.10) | copy-start | bytes 1572868
  19.3 5.1 %copy-start.7 = (bf16[128,1024]{0,1:T(8,128)(2,1)}, bf16[128,1024]{0,1:T(8,128)(2,1)S(1)}, u32[]{:S(2)}) copy-start(bf16[128,1024]{0,1:T(8,128)(2,1)S(1)} %copy.44) | copy-start | bytes 786436
  24.3 3.7 %copy-start.2 = (bf16[256,4096]{1,0:T(8,128)(2,1)S(1)}, bf16[256,4096]{1,0:T(8,128)(2,1)}, u32[]{:S(2)}) copy-start(bf16[256,4096]{1,0:T(8,128)(2,1)} %param.11) | copy-start | bytes 6291460
  24.3 4.2 %copy-start.10 = (f32[4096]{0:T(1024)S(1)}, f32[4096]{0:T(1024)}, u32[]{:S(2)}) copy-start(f32[4096]{0:T(1024)} %param.12) | copy-start | bytes 49156
  28.0 249.2 %all-gather.3.cloned.1.call-start = ((), (), s32[]{:S(2)}) async-start(), calls=%async_computation | async-start | bytes 2359296 | tf_op jit(solution)/shard_map/all_gather | solution.py:240
  28.0 1.2 copy-start.11
  28.6 10.9 %slice-start = ((s8[7340032]{0:T(1024)(128)(4,1)}), s8[4194304]{0:T(1024)(128)(4,1)S(1)}, s32[]{:S(2)}) async-start(s8[7340032]{0:T(1024)(128)(4,1)} %bitcast.97), calls=%async_computation.2 | async-start | bytes 8388608
  29.2 10.3 %copy-start.3 = (bf16[256,4096]{1,0:T(8,128)(2,1)}, bf16[256,4096]{1,0:T(8,128)(2,1)S(1)}, u32[]{:S(2)}) copy-start(bf16[256,4096]{1,0:T(8,128)(2,1)S(1)} %fusion.5) | copy-start | bytes 6291460
  29.2 10.3 %slice-start.1 = ((s8[7340032]{0:T(1024)(128)(4,1)}), s8[3145728]{0:T(1024)(128)(4,1)S(1)}, s32[]{:S(2)}) async-start(s8[7340032]{0:T(1024)(128)(4,1)} %bitcast.97), calls=%async_computation.3 | async-start | bytes 6291456
  29.2 12.7 %slice-start.2 = ((s8[7340032]{0:T(1024)(128)(4,1)}), s8[4194304]{0:T(1024)(128)(4,1)S(1)}, s32[]{:S(2)}) async-start(s8[7340032]{0:T(1024)(128)(4,1)} %bitcast.105), calls=%async_computation.4 | async-start | bytes 8388608
  36.7 174.8 %collective-permute-start.6 = (bf16[256,896]{1,0:T(8,128)(2,1)}, bf16[256,896]{1,0:T(8,128)(2,1)}, u32[]{:S(2)}, u32[]{:S(2)}) collective-permute-start(bf16[256,896]{1,0:T(8,128)(2,1)} %get-tuple-element.28), channel_id=1, source_target_pairs={{0,8},{8,16},{16,24},{24,0},{1,9},{9,17},{17,25},{25,1},{2,10},{10... | collective-permute-start | bytes 1376264 | tf_op jit(solution)/shard_map/ppermute | solution.py:157
  38.2 185.7 %collective-permute-start.7 = (bf16[256,896]{1,0:T(8,128)(2,1)}, bf16[256,896]{1,0:T(8,128)(2,1)}, u32[]{:S(2)}, u32[]{:S(2)}) collective-permute-start(bf16[256,896]{1,0:T(8,128)(2,1)} %get-tuple-element.28), channel_id=1, source_target_pairs={{0,16},{8,24},{16,0},{24,8},{1,17},{9,25},{17,1},{25,9},{2,18},{10... | collective-permute-start | bytes 1376264 | tf_op jit(solution)/shard_map/ppermute | solution.py:157
  39.5 2.5 slice-start.3
  42.0 2.4 copy-start.12
  84.1 7.4 %copy-start.1 = (bf16[256,512]{1,0:T(8,128)(2,1)S(1)}, bf16[256,512]{1,0:T(8,128)(2,1)}, u32[]{:S(2)}) copy-start(bf16[256,512]{1,0:T(8,128)(2,1)} %fusion.52.refs_0_) | copy-start | bytes 786436
  87.0 141.6 %collective-permute-start = (bf16[256,1024]{1,0:T(8,128)(2,1)}, bf16[256,1024]{1,0:T(8,128)(2,1)}, u32[]{:S(2)}, u32[]{:S(2)}) collective-permute-start(bf16[256,1024]{1,0:T(8,128)(2,1)} %get-tuple-element.25), channel_id=1, source_target_pairs={{0,8},{8,16},{16,24},{24,0},{1,9},{9,17},{17,25},{25,1},{2,10},{10... | collective-permute-start | bytes 1572872 | tf_op jit(solution)/shard_map/ppermute | solution.py:157
  88.5 140.1 %collective-permute-start.1 = (bf16[256,1024]{1,0:T(8,128)(2,1)}, bf16[256,1024]{1,0:T(8,128)(2,1)}, u32[]{:S(2)}, u32[]{:S(2)}) collective-permute-start(bf16[256,1024]{1,0:T(8,128)(2,1)} %get-tuple-element.24), channel_id=1, source_target_pairs={{0,16},{8,24},{16,0},{24,8},{1,17},{9,25},{17,1},{25,9},{2,18},{10... | collective-permute-start | bytes 1572872 | tf_op jit(solution)/shard_map/ppermute | solution.py:157
  89.9 138.7 %collective-permute-start.2 = (bf16[256,1024]{1,0:T(8,128)(2,1)}, bf16[256,1024]{1,0:T(8,128)(2,1)}, u32[]{:S(2)}, u32[]{:S(2)}) collective-permute-start(bf16[256,1024]{1,0:T(8,128)(2,1)} %get-tuple-element.23), channel_id=1, source_target_pairs={{0,24},{8,0},{16,8},{24,16},{1,25},{9,1},{17,9},{25,17},{2,26},{10... | collective-permute-start | bytes 1572872 | tf_op jit(solution)/shard_map/ppermute | solution.py:157
  186.3 3.7 %copy-start.5 = (bf16[1024,256]{1,0:T(8,128)(2,1)S(1)}, bf16[1024,256]{1,0:T(8,128)(2,1)}, u32[]{:S(2)}) copy-start(bf16[1024,256]{1,0:T(8,128)(2,1)} %copy-done.4) | copy-start | bytes 1572868
  190.0 2.7 copy-start.8
  192.7 7.8 %copy-start.9 = (bf16[1024,128]{1,0:T(8,128)(2,1)S(1)}, bf16[1024,128]{1,0:T(8,128)(2,1)}, u32[]{:S(2)}) copy-start(bf16[1024,128]{1,0:T(8,128)(2,1)} %fusion.42) | copy-start | bytes 786436
  211.5 17.2 %copy-start.6 = (bf16[256,1024]{1,0:T(8,128)(2,1)S(1)}, bf16[256,1024]{1,0:T(8,128)(2,1)}, u32[]{:S(2)}) copy-start(bf16[256,1024]{1,0:T(8,128)(2,1)} %get-tuple-element.22) | copy-start | bytes 1572868
  211.5 13.9 %collective-permute-start.8 = (bf16[256,896]{1,0:T(8,128)(2,1)}, bf16[256,896]{1,0:T(8,128)(2,1)}, u32[]{:S(2)}, u32[]{:S(2)}) collective-permute-start(bf16[256,896]{1,0:T(8,128)(2,1)} %get-tuple-element.28), channel_id=1, source_target_pairs={{0,24},{8,0},{16,8},{24,16},{1,25},{9,1},{17,9},{25,17},{2,26},{10... | collective-permute-start | bytes 1376264 | tf_op jit(solution)/shard_map/ppermute | solution.py:157
  224.0 13.6 %collective-permute-start.3 = (bf16[256,896]{1,0:T(8,128)(2,1)}, bf16[256,896]{1,0:T(8,128)(2,1)S(1)}, u32[]{:S(2)}, u32[]{:S(2)}) collective-permute-start(bf16[256,896]{1,0:T(8,128)(2,1)} %copy-done.12), channel_id=1, source_target_pairs={{0,8},{8,16},{16,24},{24,0},{1,9},{9,17},{17,25},{25,1},{2,10},{10... | collective-permute-start | bytes 1376264 | tf_op jit(solution)/shard_map/ppermute | solution.py:157
  225.4 40.0 %collective-permute-start.4 = (bf16[256,896]{1,0:T(8,128)(2,1)}, bf16[256,896]{1,0:T(8,128)(2,1)S(1)}, u32[]{:S(2)}, u32[]{:S(2)}) collective-permute-start(bf16[256,896]{1,0:T(8,128)(2,1)} %copy-done.12), channel_id=1, source_target_pairs={{0,16},{8,24},{16,0},{24,8},{1,17},{9,25},{17,1},{25,9},{2,18},{10... | collective-permute-start | bytes 1376264 | tf_op jit(solution)/shard_map/ppermute | solution.py:157
  228.6 39.7 %collective-permute-start.5 = (bf16[256,896]{1,0:T(8,128)(2,1)}, bf16[256,896]{1,0:T(8,128)(2,1)S(1)}, u32[]{:S(2)}, u32[]{:S(2)}) collective-permute-start(bf16[256,896]{1,0:T(8,128)(2,1)} %copy-done.12), channel_id=1, source_target_pairs={{0,24},{8,0},{16,8},{24,16},{1,25},{9,1},{17,9},{25,17},{2,26},{10... | collective-permute-start | bytes 1376264 | tf_op jit(solution)/shard_map/ppermute | solution.py:157
  228.7 39.6 %copy-start.13 = (bf16[256,896]{1,0:T(8,128)(2,1)S(1)}, bf16[256,896]{1,0:T(8,128)(2,1)}, u32[]{:S(2)}) copy-start(bf16[256,896]{1,0:T(8,128)(2,1)} %copy-done.12) | copy-start | bytes 1376260
Sparse Core Ops, SparseCore 0:
  28.1 42.4 all-gather.4
  84.2 28.1 all-gather.2

commit v2 on v1

--- a/solution.py
+++ b/solution.py
@@ -88,6 +88,95 @@
             pltpu.SemaphoreType.DMA((n,)),
             pltpu.SemaphoreType.DMA((n,)),
             pltpu.SemaphoreType.DMA,
+        ],
+        compiler_params=params(collective_id),
+    )(x)
+
+
+def pair_scatter_kernel(
+    axis, n, dim, src, out, own, near, sums, far, near_sems, far_sems, own_sems
+):
+    pairs = n // 2
+    me = lax.axis_index(axis)
+    chip, core = me // 2, lax.rem(me, 2)
+    partner = chip * 2 + 1 - core
+    size = out.shape[dim]
+    order = list(range(1, pairs)) + [0]
+    chips = [lax.rem(chip + k, pairs) for k in range(pairs)]
+    owns = {}
+    for k in order:
+        owns[k] = pltpu.make_async_copy(
+            part(src, dim, chips[k] * 2 + core, size), own.at[k], own_sems.at[k]
+        )
+        owns[k].start()
+    barrier = pltpu.get_barrier_semaphore()
+    for k in range(pairs):
+        peer = partner if k == 0 else chips[k] * 2 + core
+        pl.semaphore_signal(barrier, inc=1, device_id={axis: peer}, device_id_type=MESH)
+    pl.semaphore_wait(barrier, pairs)
+    nears, fars = {}, {}
+    for k in order:
+        nears[k] = pltpu.make_async_remote_copy(
+            src_ref=part(src, dim, chips[k] * 2 + 1 - core, size),
+            dst_ref=near.at[k],
+            send_sem=near_sems.at[0, k],
+            recv_sem=near_sems.at[1, k],
+            device_id={axis: partner},
+            device_id_type=MESH,
+        )
+        nears[k].start()
+    step = 32
+    for k in order:
+        owns[k].wait()
+        nears[k].wait()
+        if k == 0:
+            continue
+
+        @pl.loop(0, out.shape[0] // step)
+        def _(i):
+            rows = pl.ds(pl.multiple_of(i * step, step), step)
+            total = own[k, rows].astype(jnp.float32) + near[k, rows].astype(jnp.float32)
+            sums[k, rows] = total.astype(sums.dtype)
+
+        fars[k] = pltpu.make_async_remote_copy(
+            src_ref=sums.at[k],
+            dst_ref=far.at[k],
+            send_sem=far_sems.at[0, k],
+            recv_sem=far_sems.at[1, k],
+            device_id={axis: chips[k] * 2 + core},
+            device_id_type=MESH,
+        )
+        fars[k].start()
+    for k in range(1, pairs):
+        fars[k].wait()
+
+    @pl.loop(0, out.shape[0] // step)
+    def _(i):
+        rows = pl.ds(pl.multiple_of(i * step, step), step)
+        total = own[0, rows].astype(jnp.float32) + near[0, rows].astype(jnp.float32)
+        for k in range(1, pairs):
+            total = total + far[k, rows].astype(jnp.float32)
+        out[rows] = total.astype(out.dtype)
+
+
+def pair_scatter_sum(x, axis, dim, collective_id):
+    n = lax.axis_size(axis)
+    shape = list(x.shape)
+    shape[dim] //= n
+    held = pltpu.VMEM((n // 2, *shape), x.dtype)
+    return pl.pallas_call(
+        functools.partial(pair_scatter_kernel, axis, n, dim),
+        out_shape=jax.ShapeDtypeStruct(tuple(shape), x.dtype),
+        in_specs=[ANY],
+        out_specs=VMEM,
+        scratch_shapes=[
+            held,
+            held,
+            held,
+            held,
+            pltpu.SemaphoreType.DMA((2, n // 2)),
+            pltpu.SemaphoreType.DMA((2, n // 2)),
+            pltpu.SemaphoreType.DMA((n // 2,)),
         ],
         compiler_params=params(collective_id),
     )(x)
@@ -184,17 +273,17 @@
     per_kv = queries.shape[1] // head_dim
     score_scale = 1.0 / math.sqrt(head_dim)
 
-    kv_all = lax.all_gather(
-        jnp.concatenate([keys_in, values_in], axis=1), "wide", axis=0, tiled=True
-    )
-    keys_all, values_all = kv_all[:, :head_dim], kv_all[:, head_dim:]
+    keys_all, values_all = gather([keys_in, values_in], [("wide", 0), ("wide", 0)], 6)
 
     resid_f = residual.astype(jnp.float32)
     inv_rms = lax.rsqrt(jnp.mean(resid_f * resid_f, axis=-1, keepdims=True) + EPSILON)
     normed = (resid_f * inv_rms * norm_gain).astype(jnp.bfloat16)
 
+    core = lax.rem(wide_at, 2)
+    cols_half = cols_head // 2
+
     def normed_cols(owner):
-        return lax.dynamic_slice_in_dim(normed, owner * cols_head, cols_head, 1)
+        return lax.dynamic_slice_in_dim(normed, owner * cols_head + core * cols_half, cols_half, 1)
 
     normed_parts = [normed_cols(head_at)]
     for k in range(1, heads_n):
@@ -214,12 +303,15 @@
     partial_norm = partial_norm + lax.dot_general(
         grad_u, w_up, contract_last, preferred_element_type=jnp.float32
     )
-    gate_parts, up_parts = [grad_g], [grad_u]
+    both_grads = jnp.concatenate([grad_g, grad_u], axis=1)
+    grads_parts = [both_grads]
     for k in range(1, heads_n):
-        gate_parts.append(shifted(grad_g, "head", heads_n, k))
-        up_parts.append(shifted(grad_u, "head", heads_n, k))
-
-    grad_norm = scatter_sum(partial_norm.astype(jnp.bfloat16), "wide", 1, 1).astype(jnp.float32)
+        grads_parts.append(shifted(both_grads, "head", heads_n, k))
+
+    partial_norm, normed_parts = lax.optimization_barrier(
+        (partial_norm.astype(jnp.bfloat16), normed_parts)
+    )
+    grad_norm = pair_scatter_sum(partial_norm, "wide", 1, 1).astype(jnp.float32)
     resid_own = lax.dynamic_slice_in_dim(residual, wide_at * cols_wide, cols_wide, 1)
     normed_own = resid_own.astype(jnp.float32) * inv_rms
     gain_own = lax.dynamic_slice_in_dim(norm_gain, wide_at * cols_wide, cols_wide, 0)
@@ -235,7 +327,8 @@
     resid_grad = (
         out_own.astype(jnp.float32) + inv_rms * (grad_norm * gain_own - normed_own * mean_term)
     ).astype(jnp.bfloat16)
-    resid_cols, gain_all = gather([resid_grad, gain_part], [("head", 0), ("head", 0)], 3)
+    resid_send, grads_parts = lax.optimization_barrier((resid_grad, grads_parts))
+    resid_cols, gain_all = gather([resid_send, gain_part], [("head", 0), ("head", 0)], 3)
     grad_gain = jnp.sum(gain_all.reshape(heads_n, width), axis=0)
     grad_resid = lax.all_gather(resid_grad, "wide", axis=1, tiled=True)
 
@@ -260,7 +353,7 @@
     attn_all = lax.all_gather(attn_out, "wide", axis=0, tiled=True)
 
     heads_part = jnp.dot(resid_cols, out_proj, preferred_element_type=jnp.float32)
-    grad_heads = scatter_sum(heads_part.astype(jnp.bfloat16), "wide", 0, 4)
+    grad_heads = pair_scatter_sum(heads_part.astype(jnp.bfloat16), "wide", 0, 4)
     grad_heads = grad_heads.reshape(tok_att, per_kv, head_dim)
     dprob = jnp.einsum("thd,sd->hts", grad_heads, values_all, preferred_element_type=jnp.float32)
     delta = jnp.sum(prob * dprob, axis=-1, keepdims=True)
@@ -276,18 +369,18 @@
     grad_proj = lax.dot_general(
         resid_cols, attn_all, contract_first, preferred_element_type=jnp.float32
     ).astype(jnp.bfloat16)
-    normed_all = jnp.concatenate(normed_parts, axis=0)
+    mine = jnp.concatenate(normed_parts, axis=0)
+    other = lax.ppermute(mine, "wide", [(i, i ^ 1) for i in range(wide_n)])
+    normed_all = jnp.concatenate(
+        [jnp.where(core == 0, mine, other), jnp.where(core == 0, other, mine)], axis=1
+    )
+    grads_all = jnp.concatenate(grads_parts, axis=0)
+    hidden_dev = w_gate.shape[1]
     grad_gate = lax.dot_general(
-        normed_all,
-        jnp.concatenate(gate_parts, axis=0),
-        contract_first,
-        preferred_element_type=jnp.float32,
+        normed_all, grads_all[:, :hidden_dev], contract_first, preferred_element_type=jnp.float32
     ).astype(jnp.bfloat16)
     grad_up = lax.dot_general(
-        normed_all,
-        jnp.concatenate(up_parts, axis=0),
-        contract_first,
-        preferred_element_type=jnp.float32,
+        normed_all, grads_all[:, hidden_dev:], contract_first, preferred_element_type=jnp.float32
     ).astype(jnp.bfloat16)
     return (
         grad_resid,

time: 288 us -> 287 us (level)
  waiting for transfers between devices: 34.7 us -> 87.1 us
  Pallas kernels: 137 us -> 86.7 us
  blocking collectives: 9.86 us -> 0 us
  local copies, waits for them, and re-layouts: 10.9 us -> 19.3 us
  other arithmetic: 6.72 us -> 12.6 us
  starting transfers between devices: 12.9 us -> 7.25 us
  matrix products: 60.5 us -> 56.1 us
    pallas_call x3 -> x1, Pallas kernels: 62.6 us -> 9.18 us  [scatter_sum(): pl.pallas_call(functools.partial(scatter_sum_kernel, axis, n, dim), out_s...]
    ppermute x9 -> x6, waiting for transfers between devices: 34.7 us -> 87.1 us  [shifted(): return lax.ppermute(x, axis, [(i, (i + k) % n) for i in range(n)])]
    pallas_call x0 -> x2, Pallas kernels: none -> 34.3 us  [pair_scatter_sum(): pl.pallas_call(functools.partial(pair_scatter_kernel, axis, n, dim), out_...]
    pallas_call x2 -> x3, Pallas kernels: 74.6 us -> 43.2 us  [gather(): pl.pallas_call(functools.partial(gather_kernel, plan), out_shape=outs, in...]
    all_gather x1 -> x0, blocking collectives: 9.86 us -> none  [local(): lax.all_gather(jnp.concatenate([keys_in, values_in], axis=1), 'wide', axi...]
    unnamed x38 -> x50, local copies, waits for them, and re-layouts: 5.02 us -> 13.2 us
    ppermute x9 -> x6, starting transfers between devices: 12.8 us -> 6.98 us  [shifted(): return lax.ppermute(x, axis, [(i, (i + k) % n) for i in range(n)])]
    dot_general x1, matrix products: 2.36 us -> 5.75 us  [local(): lax.dot_general(grad_g, w_gate, contract_last, preferred_element_type=jnp...]
  transfers between devices with their start and end apart: 11 -> 9, of which waited for: 4 -> 2; matrix products, arithmetic and copies ran while one was open for 22% -> 26% of each run, Pallas kernels for 48% -> 27%
where the time goes in v2:
time: 287 us; the launch traced here: 284 us
  waiting for transfers between devices  87.1 us (30%)
  Pallas kernels  86.7 us (30%)
  matrix products  56.1 us (20%)
  local copies, waits for them, and re-layouts  19.3 us (7%)
  between operations  14.5 us (5%)
  other arithmetic  12.6 us (4%)
  starting transfers between devices  7.25 us (3%)
    ppermute x6, waiting for transfers between devices, shifted(): return lax.ppermute(x, axis, [(i, (i + k) % n) for i in range(n)])  87.1 us
    pallas_call x3, Pallas kernels, gather(): pl.pallas_call(functools.partial(gather_kernel, plan), out_shape=outs, in...  43.2 us
    pallas_call x2, Pallas kernels, pair_scatter_sum(): pl.pallas_call(functools.partial(pair_scatter_kernel, axis, n, dim), out_...  34.3 us
    unnamed x50, local copies, waits for them, and re-layouts  13.2 us
    pallas_call x1, Pallas kernels, scatter_sum(): pl.pallas_call(functools.partial(scatter_sum_kernel, axis, n, dim), out_s...  9.18 us
    dot_general x1, matrix products, local(): jnp.einsum('hts,thd->sd', dscore, query3, preferred_element_type=jnp.floa...  7.82 us
    dot_general x1, matrix products, local(): jnp.einsum('hts,sd->thd', dscore, keys_all, preferred_element_type=jnp.fl...  7.2 us
    ppermute x6, starting transfers between devices, shifted(): return lax.ppermute(x, axis, [(i, (i + k) % n) for i in range(n)])  6.98 us
  transfers between devices with their start and end apart: 9, of which 2 were waited for; matrix products, arithmetic and copies ran while one was open for 26% of the time, Pallas kernels for 27%

profile of v2, /device:TPU:8, one launch (start us, length us, event | category | flops | bytes accessed | tf_op | source)
XLA Modules:
  0.0 283.6 jit_solution(8332649131325782605)
XLA Ops:
  7.2 1.2 copy.44
  9.2 0.8 copy-done.6
  10.0 9.7 %shard_map.173 = (bf16[1024,128]{1,0:T(8,128)(2,1)S(1)}, bf16[1024,128]{1,0:T(8,128)(2,1)S(1)}) custom-call(bf16[128,128]{1,0:T(8,128)(2,1)S(1)} %copy-done.5, bf16[128,128]{1,0:T(8,128)(2,1)S(1)} %copy-done.6), custom_call_target="tpu_custom_call" | custom-call | tf_op jit(solution)/shard_map/pallas_call | solution.py:235
  19.7 0.8 dynamic_slice.31
  20.5 0.9 fusion.41
  21.4 3.4 %fusion.66 = (f32[8,128]{1,0:T(8,128)S(1)}, f32[8,128,1024]{1,2,0:T(8,128)}) fusion(pred[128,1024]{0,1:T(8,128)(4,1)S(1)} %fusion.41, bf16[128,8,128]{0,2,1:T(8,128)(2,1)S(1)} %bitcast.107, bf16[1024,128]{1,0:T(8,128)(2,1)S(1)} %get-tuple-element.35), kind=kOutput, calls=%fused_computation.100 | convolution fusion | flops 272630784 | bytes 4853760 | tf_op jit(solution)/shard_map/sub | solution.py:348
  24.8 3.4 %convolution_convert_fusion.2 = bf16[128,8,128]{2,0,1:T(8,128)(2,1)} fusion(bf16[1024,128]{1,0:T(8,128)(2,1)S(1)} %get-tuple-element.34, f32[8,128,1024]{1,2,0:T(8,128)} %get-tuple-element.57, f32[8,128]{1,0:T(8,128)S(1)} %get-tuple-element.56), kind=kOutput, calls=%fused_computation.42 | convolution fusion | flops 270663680 | bytes 4722688 | tf_op jit(solution)/shard_map/hts,sd->thd/dot_general | solution.py:351
  28.2 2.1 fusion.3
  30.3 2.4 fusion.5
  32.7 5.7 %fusion.36 = (bf16[256,896]{1,0:T(8,128)(2,1)S(1)}, f32[256,896]{1,0:T(8,128)S(1)}) fusion(bf16[256,896]{1,0:T(8,128)(2,1)} %param.15, bf16[256,4096]{1,0:T(8,128)(2,1)S(1)} %fusion.5, bf16[4096,896]{1,0:T(8,128)(2,1)} %param.13), kind=kOutput, calls=%fused_computation.49 | convolution fusion | flops 1880653824 | bytes 11272192 | tf_op jit(solution)/shard_map/dot_general | solution.py:294
  38.5 2.5 fusion.28
  41.0 1.1 pad_maximum_fusion.3
  42.1 1.6 collective-permute-start.3
  43.7 1.3 collective-permute-start.4
  44.9 1.0 constant_dynamic-slice_fusion
  46.6 3.5 %collective-permute-start.1 = (bf16[256,512]{1,0:T(8,128)(2,1)}, bf16[256,512]{1,0:T(8,128)(2,1)}, u32[]{:S(2)}, u32[]{:S(2)}) collective-permute-start(bf16[256,512]{1,0:T(8,128)(2,1)} %get-tuple-element.49), channel_id=1, source_target_pairs={{0,16},{8,24},{16,0},{24,8},{1,17},{9,25},{17,1},{25,9},{2,18},{10... | collective-permute-start | bytes 786440 | tf_op jit(solution)/shard_map/ppermute | solution.py:246
  50.0 5.7 %fusion.71 = f32[256,4096]{1,0:T(8,128)S(1)} fusion(bf16[256,896]{1,0:T(8,128)(2,1)} %copy-done.11, bf16[4096,896]{1,0:T(8,128)(2,1)} %param.13), kind=kOutput, calls=%fused_computation.101 | convolution fusion | flops 1879048192 | bytes 11993088 | tf_op jit(solution)/shard_map/dot_general | solution.py:300
  55.8 2.4 fusion.2.src
  58.3 82.2 %collective-permute-done = bf16[256,512]{1,0:T(8,128)(2,1)S(1)} collective-permute-done((bf16[256,512]{1,0:T(8,128)(2,1)}, bf16[256,512]{1,0:T(8,128)(2,1)S(1)}, u32[]{:S(2)}, u32[]{:S(2)}) %collective-permute-start) | collective-permute-done | bytes 262176 | tf_op jit(solution)/shard_map/ppermute | solution.py:246
  140.5 4.8 %collective-permute-done.1 = bf16[256,512]{1,0:T(8,128)(2,1)} collective-permute-done((bf16[256,512]{1,0:T(8,128)(2,1)}, bf16[256,512]{1,0:T(8,128)(2,1)}, u32[]{:S(2)}, u32[]{:S(2)}) %collective-permute-start.1) | collective-permute-done | bytes 262176 | tf_op jit(solution)/shard_map/ppermute | solution.py:246
  145.4 17.2 %shard_map.170 = bf16[256,512]{1,0:T(8,128)(2,1)S(1)} custom-call(bf16[256,4096]{1,0:T(8,128)(2,1)S(1)} %fusion.2.src), custom_call_target="tpu_custom_call" | custom-call | tf_op jit(solution)/shard_map/pallas_call | solution.py:167
  162.5 1.2 multiply_reduce_fusion
  163.8 4.8 %shard_map.171 = f32[64,128]{1,0:T(8,128)S(1)} custom-call(f32[8,128]{1,0:T(8,128)S(1)} %fusion.56.refs_0_), custom_call_target="tpu_custom_call" | custom-call | tf_op jit(solution)/shard_map/pallas_call | solution.py:235
  168.6 1.0 constant_dynamic-update-slice_fusion.3
  169.6 1.0 constant_dynamic-update-slice_fusion.2
  170.5 1.0 constant_dynamic-update-slice_fusion.1
  171.5 1.0 constant_dynamic-update-slice_fusion
  172.7 1.9 fusion.40.refs_0_
  174.7 0.9 copy-done.2
  175.7 28.8 %shard_map.172 = (bf16[1024,512]{1,0:T(8,128)(2,1)S(1)}, f32[128,128]{1,0:T(8,128)S(1)}) custom-call(bf16[256,512]{1,0:T(8,128)(2,1)S(1)} %copy-done.2, f32[32,128]{1,0:T(8,128)S(1)} %reshape.109.refs_1_), custom_call_target="tpu_custom_call" | custom-call | tf_op jit(solution)/shard_map/pallas_call | solution.py:235
  204.5 1.3 convolution_convert_fusion.src
  205.7 17.1 %shard_map.174 = bf16[128,1024]{1,0:T(8,128)(2,1)S(1)} custom-call(bf16[1024,1024]{1,0:T(8,128)(2,1)S(1)} %convolution_convert_fusion.src), custom_call_target="tpu_custom_call" | custom-call | tf_op jit(solution)/shard_map/pallas_call | solution.py:167
  223.0 2.9 %fusion.30 = bf16[1024,128]{1,0:T(8,128)(2,1)S(1)} fusion(bf16[128,8,128]{0,2,1:T(8,128)(2,1)S(1)} %bitcast.104, f32[8,128,1024]{1,2,0:T(8,128)} %get-tuple-element.57, f32[8,128]{1,0:T(8,128)S(1)} %get-tuple-element.56), kind=kOutput, calls=%fused_computation.39 | convolution fusion | flops 270663680 | bytes 4722688 | tf_op jit(solution)/shard_map/hts,thd->sd/dot_general | solution.py:364
  226.0 2.7 fusion.53
  228.7 7.8 %fusion.31 = bf16[1024,128]{1,0:T(8,128)(2,1)} fusion(bf16[128,8,128]{0,2,1:T(8,128)(2,1)S(1)} %bitcast.108, f32[1024,128,8]{1,0,2:T(8,128)} %fusion.53, f32[8,128,1024]{1,2,0:T(8,128)} %get-tuple-element.57, f32[8,128]{1,0:T(8,128)S(1)} %get-tuple-element.56), kind=kOutput, calls=%fused_computation.40 | convolution fusion | flops 275908608 | bytes 8916992 | tf_op jit(solution)/shard_map/hts,thd->sd/dot_general | solution.py:363
  236.5 1.0 pad_maximum_fusion.4.src
  237.5 9.2 %shard_map.175 = bf16[128,256]{1,0:T(8,128)(2,1)S(1)} custom-call(bf16[1024,256]{1,0:T(8,128)(2,1)S(1)} %pad_maximum_fusion.4.src), custom_call_target="tpu_custom_call" | custom-call | tf_op jit(solution)/shard_map/pallas_call | solution.py:81
  246.7 7.2 %fusion.32 = bf16[128,8,128]{2,0,1:T(8,128)(2,1)S(1)} fusion(f32[1024,128,8]{1,0,2:T(8,128)} %fusion.53, bf16[1024,128]{1,0:T(8,128)(2,1)S(1)} %copy-done.8, f32[8,128,1024]{1,2,0:T(8,128)} %get-tuple-element.57, f32[8,128]{1,0:T(8,128)S(1)} %get-tuple-element.56), kind=kOutput, calls=%fused_computation.41 | convolution fusion | flops 275908608 | bytes 8916992 | tf_op jit(solution)/shard_map/hts,sd->thd/dot_general | solution.py:361
  254.6 0.8 copy.31
  256.1 1.2 constant_dynamic-update-slice_fusion.7
  257.3 1.2 constant_dynamic-update-slice_fusion.6
  258.5 1.2 constant_dynamic-update-slice_fusion.5
  259.8 1.2 constant_dynamic-update-slice_fusion.4
  261.0 1.4 broadcast_select_fusion.1
  262.4 3.6 %fusion.20 = bf16[1024,896]{1,0:T(8,128)(2,1)} fusion(bf16[1024,1792]{1,0:T(8,128)(2,1)S(1)} %constant_dynamic-update-slice_fusion.4, bf16[1024,512]{1,0:T(8,128)(2,1)S(1)} %get-tuple-element.47, bf16[1024,512]{1,0:T(8,128)(2,1)S(1)} %get-tuple-element.46), kind=kOutput, calls=%fused_computation.30 | convolution fusion | flops 1884160000 | bytes 5767168 | tf_op jit(solution)/shard_map/dot_general | solution.py:379
  266.0 3.6 %fusion.23 = bf16[1024,896]{1,0:T(8,128)(2,1)} fusion(bf16[1024,1792]{1,0:T(8,128)(2,1)S(1)} %constant_dynamic-update-slice_fusion.4, bf16[1024,512]{1,0:T(8,128)(2,1)S(1)} %get-tuple-element.47, bf16[1024,512]{1,0:T(8,128)(2,1)S(1)} %get-tuple-element.46), kind=kOutput, calls=%fused_computation.31 | convolution fusion | flops 1884160000 | bytes 5767168 | tf_op jit(solution)/shard_map/dot_general | solution.py:382
  269.7 4.0 %convolution_convert_fusion.1 = bf16[512,1024]{1,0:T(8,128)(2,1)} fusion(bf16[1024,512]{1,0:T(8,128)(2,1)S(1)} %get-tuple-element.33, bf16[1024,1024]{0,1:T(8,128)(2,1)} %all-gather.5.cloned.1.call-done), kind=kOutput, calls=%fused_computation.32 | convolution fusion | flops 1074266112 | bytes 4194304 | tf_op jit(solution)/shard_map/dot_general | solution.py:369
  273.6 3.1 %copy.53 = bf16[256,4096]{1,0:T(8,128)(2,1)} copy(bf16[256,4096]{1,0:T(8,128)(2,1)} %all-gather.3.cloned.1.call-done) | data formatting | bytes 4194304
  (70 shorter events, 3.4 us)
Async XLA Ops:
  7.2 197.3 %copy-start = (bf16[512,1024]{1,0:T(8,128)(2,1)S(1)}, bf16[512,1024]{1,0:T(8,128)(2,1)}, u32[]{:S(2)}) copy-start(bf16[512,1024]{1,0:T(8,128)(2,1)} %param.17) | copy-start | bytes 3145732
  7.2 262.5 %all-gather.5.cloned.1.call-start = ((), (), s32[]{:S(2)}) async-start(), calls=%async_computation.1 | async-start | bytes 2359296 | tf_op jit(solution)/shard_map/all_gather | solution.py:353
  8.4 0.8 copy-start.5
  9.2 0.8 copy-start.6
  10.0 18.2 %copy-start.12 = (bf16[128,1024]{0,1:T(8,128)(2,1)}, bf16[128,1024]{0,1:T(8,128)(2,1)S(1)}, u32[]{:S(2)}) copy-start(bf16[128,1024]{0,1:T(8,128)(2,1)S(1)} %copy.44) | copy-start | bytes 786436
  19.7 8.5 %copy-start.3 = (bf16[1024,128]{1,0:T(8,128)(2,1)}, bf16[1024,128]{1,0:T(8,128)(2,1)S(1)}, u32[]{:S(2)}) copy-start(bf16[1024,128]{1,0:T(8,128)(2,1)S(1)} %get-tuple-element.34) | copy-start | bytes 786436
  19.7 8.5 %copy-start.7 = (bf16[1024,128]{1,0:T(8,128)(2,1)}, bf16[1024,128]{1,0:T(8,128)(2,1)S(1)}, u32[]{:S(2)}) copy-start(bf16[1024,128]{1,0:T(8,128)(2,1)S(1)} %get-tuple-element.35) | copy-start | bytes 786436
  24.7 5.6 %copy-start.15 = (f32[4096]{0:T(1024)S(1)}, f32[4096]{0:T(1024)}, u32[]{:S(2)}) copy-start(f32[4096]{0:T(1024)} %param.12) | copy-start | bytes 49156
  28.2 245.4 %all-gather.3.cloned.1.call-start = ((), (), s32[]{:S(2)}) async-start(), calls=%async_computation | async-start | bytes 2359296 | tf_op jit(solution)/shard_map/all_gather | solution.py:333
  30.3 8.1 %slice-start = ((s8[7340032]{0:T(1024)(128)(4,1)}), s8[4194304]{0:T(1024)(128)(4,1)S(1)}, s32[]{:S(2)}) async-start(s8[7340032]{0:T(1024)(128)(4,1)} %bitcast.100), calls=%async_computation.2 | async-start | bytes 8388608
  32.7 5.7 %slice-start.1 = ((s8[7340032]{0:T(1024)(128)(4,1)}), s8[3145728]{0:T(1024)(128)(4,1)S(1)}, s32[]{:S(2)}) async-start(s8[7340032]{0:T(1024)(128)(4,1)} %bitcast.100), calls=%async_computation.3 | async-start | bytes 6291456
  32.7 5.7 %copy-start.16 = (bf16[256,896]{1,0:T(8,128)(2,1)S(1)}, bf16[256,896]{1,0:T(8,128)(2,1)}, u32[]{:S(2)}) copy-start(bf16[256,896]{1,0:T(8,128)(2,1)} %param.15) | copy-start | bytes 1376260
  38.4 2.6 copy-start.9
  41.0 1.1 copy-start.11
  42.1 132.6 %collective-permute-start.3 = (bf16[256,1792]{1,0:T(8,128)(2,1)}, bf16[256,1792]{1,0:T(8,128)(2,1)}, u32[]{:S(2)}, u32[]{:S(2)}) collective-permute-start(bf16[256,1792]{1,0:T(8,128)(2,1)} %pad_maximum_fusion.3), channel_id=1, source_target_pairs={{0,8},{8,16},{16,24},{24,0},{1,9},{9,17},{17,25},{25,1},{2,10},{10... | collective-permute-start | bytes 2752520 | tf_op jit(solution)/shard_map/ppermute | solution.py:246
  43.7 131.0 %collective-permute-start.4 = (bf16[256,1792]{1,0:T(8,128)(2,1)}, bf16[256,1792]{1,0:T(8,128)(2,1)}, u32[]{:S(2)}, u32[]{:S(2)}) collective-permute-start(bf16[256,1792]{1,0:T(8,128)(2,1)} %pad_maximum_fusion.3), channel_id=1, source_target_pairs={{0,16},{8,24},{16,0},{24,8},{1,17},{9,25},{17,1},{25,9},{2,18},{10... | collective-permute-start | bytes 2752520 | tf_op jit(solution)/shard_map/ppermute | solution.py:246
  45.9 94.6 %collective-permute-start = (bf16[256,512]{1,0:T(8,128)(2,1)}, bf16[256,512]{1,0:T(8,128)(2,1)S(1)}, u32[]{:S(2)}, u32[]{:S(2)}) collective-permute-start(bf16[256,512]{1,0:T(8,128)(2,1)} %get-tuple-element.50), channel_id=1, source_target_pairs={{0,8},{8,16},{16,24},{24,0},{1,9},{9,17},{17,25},{25,1},{2,10},{10... | collective-permute-start | bytes 786440 | tf_op jit(solution)/shard_map/ppermute | solution.py:246
  46.6 98.8 %collective-permute-start.1 = (bf16[256,512]{1,0:T(8,128)(2,1)}, bf16[256,512]{1,0:T(8,128)(2,1)}, u32[]{:S(2)}, u32[]{:S(2)}) collective-permute-start(bf16[256,512]{1,0:T(8,128)(2,1)} %get-tuple-element.49), channel_id=1, source_target_pairs={{0,16},{8,24},{16,0},{24,8},{1,17},{9,25},{17,1},{25,9},{2,18},{10... | collective-permute-start | bytes 786440 | tf_op jit(solution)/shard_map/ppermute | solution.py:246
  50.0 5.8 %slice-start.2 = ((s8[7340032]{0:T(1024)(128)(4,1)}), s8[4194304]{0:T(1024)(128)(4,1)S(1)}, s32[]{:S(2)}) async-start(s8[7340032]{0:T(1024)(128)(4,1)} %bitcast.102), calls=%async_computation.4 | async-start | bytes 8388608
  50.0 5.8 %slice-start.3 = ((s8[7340032]{0:T(1024)(128)(4,1)}), s8[3145728]{0:T(1024)(128)(4,1)S(1)}, s32[]{:S(2)}) async-start(s8[7340032]{0:T(1024)(128)(4,1)} %bitcast.102), calls=%async_computation.5 | async-start | bytes 6291456
  50.0 5.8 %copy-start.10 = (bf16[256,896]{1,0:T(8,128)(2,1)S(1)}, bf16[256,896]{1,0:T(8,128)(2,1)}, u32[]{:S(2)}) copy-start(bf16[256,896]{1,0:T(8,128)(2,1)} %copy-done.9) | copy-start | bytes 1376260
  50.0 95.3 %collective-permute-start.2 = (bf16[256,512]{1,0:T(8,128)(2,1)}, bf16[256,512]{1,0:T(8,128)(2,1)}, u32[]{:S(2)}, u32[]{:S(2)}) collective-permute-start(bf16[256,512]{1,0:T(8,128)(2,1)} %get-tuple-element.48), channel_id=1, source_target_pairs={{0,24},{8,0},{16,8},{24,16},{1,25},{9,1},{17,9},{25,17},{2,26},{10... | collective-permute-start | bytes 786440 | tf_op jit(solution)/shard_map/ppermute | solution.py:246
  140.5 4.8 %copy-start.14 = (bf16[256,512]{1,0:T(8,128)(2,1)}, bf16[256,512]{1,0:T(8,128)(2,1)S(1)}, u32[]{:S(2)}) copy-start(bf16[256,512]{1,0:T(8,128)(2,1)S(1)} %collective-permute-done) | copy-start | bytes 786436
  140.5 34.2 %collective-permute-start.5 = (bf16[256,1792]{1,0:T(8,128)(2,1)}, bf16[256,1792]{1,0:T(8,128)(2,1)}, u32[]{:S(2)}, u32[]{:S(2)}) collective-permute-start(bf16[256,1792]{1,0:T(8,128)(2,1)} %pad_maximum_fusion.3), channel_id=1, source_target_pairs={{0,24},{8,0},{16,8},{24,16},{1,25},{9,1},{17,9},{25,17},{2,26},{10... | collective-permute-start | bytes 2752520 | tf_op jit(solution)/shard_map/ppermute | solution.py:246
  172.5 88.5 %collective-permute-start.6 = (bf16[1024,512]{1,0:T(8,128)(2,1)S(1)}, bf16[1024,512]{1,0:T(8,128)(2,1)}, u32[]{:S(2)}, u32[]{:S(2)}) collective-permute-start(bf16[1024,512]{1,0:T(8,128)(2,1)S(1)} %constant_dynamic-update-slice_fusion), channel_id=1, source_target_pairs={{0,1},{1,0},{2,3},{3,2},{4,5},{5,4},{6,7},{7,6},{8,9},{9,8},{10,11... | collective-permute-start | bytes 3145736 | tf_op jit(solution)/shard_map/ppermute | solution.py:373
  174.7 1.0 copy-start.2
  223.0 3.0 %copy-start.4 = (bf16[1024,128]{1,0:T(8,128)(2,1)S(1)}, bf16[1024,128]{1,0:T(8,128)(2,1)}, u32[]{:S(2)}) copy-start(bf16[1024,128]{1,0:T(8,128)(2,1)} %copy-done.3) | copy-start | bytes 786436
  226.0 2.7 copy-start.13
  228.7 18.0 %copy-start.8 = (bf16[1024,128]{1,0:T(8,128)(2,1)S(1)}, bf16[1024,128]{1,0:T(8,128)(2,1)}, u32[]{:S(2)}) copy-start(bf16[1024,128]{1,0:T(8,128)(2,1)} %copy-done.7) | copy-start | bytes 786436
  269.7 7.1 %copy-start.1 = (bf16[512,1024]{1,0:T(8,128)(2,1)S(1)}, bf16[512,1024]{1,0:T(8,128)(2,1)}, u32[]{:S(2)}) copy-start(bf16[512,1024]{1,0:T(8,128)(2,1)} %param.17) | copy-start | bytes 3145732
Sparse Core Ops, SparseCore 0:
  28.3 29.2 all-gather.4
  174.8 30.0 all-gather.2

commit v3 on v2

--- a/solution.py
+++ b/solution.py
@@ -279,11 +279,12 @@
     inv_rms = lax.rsqrt(jnp.mean(resid_f * resid_f, axis=-1, keepdims=True) + EPSILON)
     normed = (resid_f * inv_rms * norm_gain).astype(jnp.bfloat16)
 
-    core = lax.rem(wide_at, 2)
-    cols_half = cols_head // 2
+    cols_piece = cols_head // wide_n
 
     def normed_cols(owner):
-        return lax.dynamic_slice_in_dim(normed, owner * cols_head + core * cols_half, cols_half, 1)
+        return lax.dynamic_slice_in_dim(
+            normed, owner * cols_head + wide_at * cols_piece, cols_piece, 1
+        )
 
     normed_parts = [normed_cols(head_at)]
     for k in range(1, heads_n):
@@ -303,15 +304,13 @@
     partial_norm = partial_norm + lax.dot_general(
         grad_u, w_up, contract_last, preferred_element_type=jnp.float32
     )
-    both_grads = jnp.concatenate([grad_g, grad_u], axis=1)
-    grads_parts = [both_grads]
+    gate_send, normed_parts = lax.optimization_barrier((grad_g, normed_parts))
+    gate_parts = [grad_g]
     for k in range(1, heads_n):
-        grads_parts.append(shifted(both_grads, "head", heads_n, k))
-
-    partial_norm, normed_parts = lax.optimization_barrier(
-        (partial_norm.astype(jnp.bfloat16), normed_parts)
-    )
-    grad_norm = pair_scatter_sum(partial_norm, "wide", 1, 1).astype(jnp.float32)
+        gate_parts.append(shifted(gate_send, "head", heads_n, k))
+    normed_all = lax.all_gather(jnp.concatenate(normed_parts, axis=0), "wide", axis=0)
+    grad_norm = pair_scatter_sum(partial_norm.astype(jnp.bfloat16), "wide", 1, 1)
+    grad_norm = grad_norm.astype(jnp.float32)
     resid_own = lax.dynamic_slice_in_dim(residual, wide_at * cols_wide, cols_wide, 1)
     normed_own = resid_own.astype(jnp.float32) * inv_rms
     gain_own = lax.dynamic_slice_in_dim(norm_gain, wide_at * cols_wide, cols_wide, 0)
@@ -327,8 +326,12 @@
     resid_grad = (
         out_own.astype(jnp.float32) + inv_rms * (grad_norm * gain_own - normed_own * mean_term)
     ).astype(jnp.bfloat16)
-    resid_send, grads_parts = lax.optimization_barrier((resid_grad, grads_parts))
+    resid_send, gate_parts = lax.optimization_barrier((resid_grad, gate_parts))
     resid_cols, gain_all = gather([resid_send, gain_part], [("head", 0), ("head", 0)], 3)
+    up_send, resid_cols = lax.optimization_barrier((grad_u, resid_cols))
+    up_parts = [grad_u]
+    for k in range(1, heads_n):
+        up_parts.append(shifted(up_send, "head", heads_n, k))
     grad_gain = jnp.sum(gain_all.reshape(heads_n, width), axis=0)
     grad_resid = lax.all_gather(resid_grad, "wide", axis=1, tiled=True)
 
@@ -369,19 +372,18 @@
     grad_proj = lax.dot_general(
         resid_cols, attn_all, contract_first, preferred_element_type=jnp.float32
     ).astype(jnp.bfloat16)
-    mine = jnp.concatenate(normed_parts, axis=0)
-    other = lax.ppermute(mine, "wide", [(i, i ^ 1) for i in range(wide_n)])
-    normed_all = jnp.concatenate(
-        [jnp.where(core == 0, mine, other), jnp.where(core == 0, other, mine)], axis=1
-    )
-    grads_all = jnp.concatenate(grads_parts, axis=0)
-    hidden_dev = w_gate.shape[1]
-    grad_gate = lax.dot_general(
-        normed_all, grads_all[:, :hidden_dev], contract_first, preferred_element_type=jnp.float32
-    ).astype(jnp.bfloat16)
-    grad_up = lax.dot_general(
-        normed_all, grads_all[:, hidden_dev:], contract_first, preferred_element_type=jnp.float32
-    ).astype(jnp.bfloat16)
+    contract_tokens = (((1,), (0,)), ((), ()))
+    grad_gate, grad_up = (
+        lax.dot_general(
+            normed_all,
+            jnp.concatenate(parts, axis=0),
+            contract_tokens,
+            preferred_element_type=jnp.float32,
+        )
+        .astype(jnp.bfloat16)
+        .reshape(cols_head, -1)
+        for parts in (gate_parts, up_parts)
+    )
     return (
         grad_resid,
         grad_gain,

time: 287 us -> 236 us (0.82)
  waiting for transfers between devices: 87.1 us -> 42.8 us
  local copies, waits for them, and re-layouts: 19.3 us -> 9.36 us
  starting transfers between devices: 7.25 us -> 12.3 us
    ppermute x6 -> x9, waiting for transfers between devices: 87.1 us -> 42.7 us  [shifted(): return lax.ppermute(x, axis, [(i, (i + k) % n) for i in range(n)])]
    unnamed x50 -> x38, local copies, waits for them, and re-layouts: 13.2 us -> 5.5 us
    ppermute x6 -> x9, starting transfers between devices: 6.98 us -> 12 us  [shifted(): return lax.ppermute(x, axis, [(i, (i + k) % n) for i in range(n)])]
    dot_general x2, matrix products: 7.24 us -> 10.7 us  [local(): lax.dot_general(normed_all, jnp.concatenate(parts, axis=0), contract_toke...]
    dot_general x1, matrix products: 5.75 us -> 2.44 us  [local(): lax.dot_general(grad_g, w_gate, contract_last, preferred_element_type=jnp...]
  transfers between devices with their start and end apart: 9 -> 12, of which waited for: 2 -> 5; matrix products, arithmetic and copies ran while one was open for 26% -> 25% of each run, Pallas kernels for 27% -> 33%
where the time goes in v3:
time: 236 us; the launch traced here: 232 us
  Pallas kernels  85.5 us (36%)
  matrix products  58.2 us (25%)
  waiting for transfers between devices  42.8 us (18%)
  between operations  14.1 us (6%)
  starting transfers between devices  12.3 us (5%)
  other arithmetic  10.1 us (4%)
  local copies, waits for them, and re-layouts  9.36 us (4%)
    ppermute x9, waiting for transfers between devices, shifted(): return lax.ppermute(x, axis, [(i, (i + k) % n) for i in range(n)])  42.7 us
    pallas_call x3, Pallas kernels, gather(): pl.pallas_call(functools.partial(gather_kernel, plan), out_shape=outs, in...  41.2 us
    pallas_call x2, Pallas kernels, pair_scatter_sum(): pl.pallas_call(functools.partial(pair_scatter_kernel, axis, n, dim), out_...  35.7 us
    ppermute x9, starting transfers between devices, shifted(): return lax.ppermute(x, axis, [(i, (i + k) % n) for i in range(n)])  12 us
    dot_general x2, matrix products, local(): lax.dot_general(normed_all, jnp.concatenate(parts, axis=0), contract_toke...  10.7 us
    pallas_call x1, Pallas kernels, scatter_sum(): pl.pallas_call(functools.partial(scatter_sum_kernel, axis, n, dim), out_s...  8.61 us
    dot_general x1, matrix products, local(): gate_pre = jnp.dot(normed, w_gate, preferred_element_type=jnp.float32)  7.2 us
    dot_general x1, matrix products, local(): jnp.einsum('hts,sd->thd', dscore, keys_all, preferred_element_type=jnp.fl...  7.2 us
  transfers between devices with their start and end apart: 12, of which 5 were waited for; matrix products, arithmetic and copies ran while one was open for 25% of the time, Pallas kernels for 33%

profile of v3, /device:TPU:8, one launch (start us, length us, event | category | flops | bytes accessed | tf_op | source)
XLA Modules:
  0.0 232.3 jit_solution(1235923658552106038)
XLA Ops:
  7.2 1.2 copy.61
  8.5 0.8 copy-done.2
  9.2 0.8 copy-done.3
  10.0 9.7 %shard_map.173 = (bf16[1024,128]{1,0:T(8,128)(2,1)S(1)}, bf16[1024,128]{1,0:T(8,128)(2,1)S(1)}) custom-call(bf16[128,128]{1,0:T(8,128)(2,1)S(1)} %copy-done.2, bf16[128,128]{1,0:T(8,128)(2,1)S(1)} %copy-done.3), custom_call_target="tpu_custom_call" | custom-call | tf_op jit(solution)/shard_map/pallas_call | solution.py:235
  19.6 0.8 dynamic_slice.31
  20.4 0.9 fusion.47
  21.3 3.4 %fusion.72 = (f32[8,128]{1,0:T(8,128)S(1)}, f32[8,128,1024]{1,2,0:T(8,128)}) fusion(pred[128,1024]{0,1:T(8,128)(4,1)S(1)} %fusion.47, bf16[128,8,128]{0,2,1:T(8,128)(2,1)S(1)} %bitcast.120, bf16[1024,128]{1,0:T(8,128)(2,1)S(1)} %get-tuple-element.39), kind=kOutput, calls=%fused_computation.101 | convolution fusion | flops 272630784 | bytes 4853760 | tf_op jit(solution)/shard_map/sub | solution.py:351
  24.7 3.4 %convolution_convert_fusion.2 = bf16[128,8,128]{2,0,1:T(8,128)(2,1)} fusion(bf16[1024,128]{1,0:T(8,128)(2,1)S(1)} %get-tuple-element.38, f32[8,128,1024]{1,2,0:T(8,128)} %get-tuple-element.67, f32[8,128]{1,0:T(8,128)S(1)} %get-tuple-element.66), kind=kOutput, calls=%fused_computation.53 | convolution fusion | flops 270663680 | bytes 4722688 | tf_op jit(solution)/shard_map/hts,sd->thd/dot_general | solution.py:354
  28.3 2.1 fusion.3
  30.4 2.5 %fusion.5 = bf16[256,4096]{1,0:T(8,128)(2,1)S(1)} fusion(bf16[256,4096]{1,0:T(8,128)(2,1)} %param.11, f32[4096]{0:T(1024)S(1)} %copy-done.6, f32[256]{0:T(256)S(1)} %add_rsqrt_fusion), kind=kLoop, calls=%fused_computation.8 | loop fusion | flops 4194304 | bytes 4211712 | tf_op jit(solution)/shard_map/convert_element_type | solution.py:280
  33.0 7.2 %fusion.42 = (bf16[256,896]{1,0:T(8,128)(2,1)}, f32[256,896]{1,0:T(8,128)S(1)}) fusion(bf16[256,896]{1,0:T(8,128)(2,1)S(1)} %copy-done.8, bf16[256,4096]{1,0:T(8,128)(2,1)S(1)} %fusion.5, bf16[4096,896]{1,0:T(8,128)(2,1)} %param.13), kind=kOutput, calls=%fused_computation.58 | convolution fusion | flops 1880653824 | bytes 11272192 | tf_op jit(solution)/shard_map/dot_general | solution.py:295
  40.2 2.5 %fusion.34 = bf16[256,896]{1,0:T(8,128)(2,1)S(1)} fusion(bf16[256,4096]{1,0:T(8,128)(2,1)S(1)} %fusion.5, bf16[4096,896]{1,0:T(8,128)(2,1)S(1)} %bitcast.116, bf16[256,896]{1,0:T(8,128)(2,1)S(1)} %copy-done.8, f32[256,896]{1,0:T(8,128)S(1)} %get-tuple-element.65), kind=kOutput, calls=%fused_computation.47 | convolution fusion | flops 1881571328 | bytes 11272192 | tf_op jit(solution)/shard_map/dot_general | solution.py:296
  42.7 2.4 %fusion.77 = f32[256,4096]{1,0:T(8,128)S(1)} fusion(bf16[256,896]{1,0:T(8,128)(2,1)S(1)} %fusion.34, bf16[4096,896]{1,0:T(8,128)(2,1)S(1)} %bitcast.124), kind=kOutput, calls=%fused_computation.102 | convolution fusion | flops 1879048192 | bytes 11993088 | tf_op jit(solution)/shard_map/dot_general | solution.py:301
  45.2 3.5 %fusion.2.src = bf16[256,4096]{1,0:T(8,128)(2,1)S(1)} fusion(f32[256,4096]{1,0:T(8,128)S(1)} %fusion.77, bf16[256,896]{1,0:T(8,128)(2,1)} %get-tuple-element.36, bf16[4096,896]{1,0:T(8,128)(2,1)S(1)} %bitcast.116), kind=kOutput, calls=%fused_computation.5 | convolution fusion | flops 1881145344 | bytes 14090240 | tf_op jit(solution)/shard_map/dot_general | solution.py:304
  48.7 18.4 %shard_map.170 = bf16[256,512]{1,0:T(8,128)(2,1)S(1)} custom-call(bf16[256,4096]{1,0:T(8,128)(2,1)S(1)} %fusion.2.src), custom_call_target="tpu_custom_call" | custom-call | tf_op jit(solution)/shard_map/pallas_call | solution.py:167
  67.2 1.2 multiply_reduce_fusion
  68.5 4.8 %shard_map.171 = f32[64,128]{1,0:T(8,128)S(1)} custom-call(f32[8,128]{1,0:T(8,128)S(1)} %fusion.62.refs_0_), custom_call_target="tpu_custom_call" | custom-call | tf_op jit(solution)/shard_map/pallas_call | solution.py:235
  73.3 2.0 fusion.46.refs_0_
  75.4 1.0 constant_dynamic-slice_fusion
  76.4 1.5 collective-permute-start
  77.9 1.4 collective-permute-start.1
  79.3 1.5 collective-permute-start.2
  80.9 3.1 %collective-permute-done.1 = bf16[256,128]{1,0:T(8,128)(2,1)S(1)} collective-permute-done((bf16[256,128]{1,0:T(8,128)(2,1)S(1)}, bf16[256,128]{1,0:T(8,128)(2,1)S(1)}, u32[]{:S(2)}, u32[]{:S(2)}) %collective-permute-start.1) | collective-permute-done | bytes 65568 | tf_op jit(solution)/shard_map/ppermute | solution.py:246
  84.0 1.7 collective-permute-done.2
  85.6 0.7 pad_maximum_fusion.1
  86.5 2.7 %collective-permute-start.4 = (bf16[256,896]{1,0:T(8,128)(2,1)S(1)}, bf16[256,896]{1,0:T(8,128)(2,1)S(1)}, u32[]{:S(2)}, u32[]{:S(2)}) collective-permute-start(bf16[256,896]{1,0:T(8,128)(2,1)S(1)} %fusion.34), channel_id=1, source_target_pairs={{0,16},{8,24},{16,0},{24,8},{1,17},{9,25},{17,1},{25,9},{2,18},{10... | collective-permute-start | bytes 1376264 | tf_op jit(solution)/shard_map/ppermute | solution.py:246
  89.1 1.0 collective-permute-start.5
  90.1 9.7 %collective-permute-done.3 = bf16[256,896]{1,0:T(8,128)(2,1)S(1)} collective-permute-done((bf16[256,896]{1,0:T(8,128)(2,1)S(1)}, bf16[256,896]{1,0:T(8,128)(2,1)S(1)}, u32[]{:S(2)}, u32[]{:S(2)}) %collective-permute-start.3) | collective-permute-done | bytes 458784 | tf_op jit(solution)/shard_map/ppermute | solution.py:246
  99.8 26.3 %collective-permute-done.4 = bf16[256,896]{1,0:T(8,128)(2,1)S(1)} collective-permute-done((bf16[256,896]{1,0:T(8,128)(2,1)S(1)}, bf16[256,896]{1,0:T(8,128)(2,1)S(1)}, u32[]{:S(2)}, u32[]{:S(2)}) %collective-permute-start.4) | collective-permute-done | bytes 458784 | tf_op jit(solution)/shard_map/ppermute | solution.py:246
  126.1 0.8 copy-done.13
  126.9 2.0 collective-permute-done.5
  128.9 1.0 copy-done.1
  129.8 26.7 %shard_map.172 = (bf16[1024,512]{1,0:T(8,128)(2,1)S(1)}, f32[128,128]{1,0:T(8,128)S(1)}) custom-call(bf16[256,512]{1,0:T(8,128)(2,1)S(1)} %copy-done.1, f32[32,128]{1,0:T(8,128)S(1)} %reshape.115.refs_1_), custom_call_target="tpu_custom_call" | custom-call | tf_op jit(solution)/shard_map/pallas_call | solution.py:235
  156.6 0.7 collective-permute-start.6
  157.2 3.0 %collective-permute-start.7 = (bf16[256,896]{1,0:T(8,128)(2,1)}, bf16[256,896]{1,0:T(8,128)(2,1)}, u32[]{:S(2)}, u32[]{:S(2)}) collective-permute-start(bf16[256,896]{1,0:T(8,128)(2,1)} %get-tuple-element.36), channel_id=1, source_target_pairs={{0,16},{8,24},{16,0},{24,8},{1,17},{9,25},{17,1},{25,9},{2,18},{10... | collective-permute-start | bytes 1376264 | tf_op jit(solution)/shard_map/ppermute | solution.py:246
  160.3 1.3 convolution_convert_fusion.src
  161.6 17.3 %shard_map.174 = bf16[128,1024]{1,0:T(8,128)(2,1)S(1)} custom-call(bf16[1024,1024]{1,0:T(8,128)(2,1)S(1)} %convolution_convert_fusion.src), custom_call_target="tpu_custom_call" | custom-call | tf_op jit(solution)/shard_map/pallas_call | solution.py:167
  179.0 2.7 %fusion.59 = f32[1024,128,8]{1,0,2:T(8,128)} fusion(bf16[128,8,128]{0,2,1:T(8,128)(2,1)S(1)} %bitcast.117, bf16[1024,128]{1,0:T(8,128)(2,1)S(1)} %get-tuple-element.38), kind=kOutput, calls=%fused_computation.78 | convolution fusion | flops 268435456 | bytes 4718592 | tf_op jit(solution)/shard_map/thd,sd->hts/dot_general | solution.py:361
  181.7 7.1 %fusion.37 = bf16[1024,128]{1,0:T(8,128)(2,1)S(1)} fusion(bf16[128,8,128]{0,2,1:T(8,128)(2,1)S(1)} %bitcast.121, f32[1024,128,8]{1,0,2:T(8,128)} %fusion.59, f32[8,128,1024]{1,2,0:T(8,128)} %get-tuple-element.67, f32[8,128]{1,0:T(8,128)S(1)} %get-tuple-element.66), kind=kOutput, calls=%fused_computation.51 | convolution fusion | flops 275908608 | bytes 8916992 | tf_op jit(solution)/shard_map/hts,thd->sd/dot_general | solution.py:366
  188.8 2.9 %fusion.36 = bf16[1024,128]{1,0:T(8,128)(2,1)S(1)} fusion(bf16[128,8,128]{0,2,1:T(8,128)(2,1)S(1)} %bitcast.118, f32[8,128,1024]{1,2,0:T(8,128)} %get-tuple-element.67, f32[8,128]{1,0:T(8,128)S(1)} %get-tuple-element.66), kind=kOutput, calls=%fused_computation.50 | convolution fusion | flops 270663680 | bytes 4722688 | tf_op jit(solution)/shard_map/hts,thd->sd/dot_general | solution.py:367
  191.8 8.6 %shard_map.175 = bf16[128,256]{1,0:T(8,128)(2,1)S(1)} custom-call(bf16[1024,256]{1,0:T(8,128)(2,1)S(1)} %pad_maximum_fusion.src), custom_call_target="tpu_custom_call" | custom-call | tf_op jit(solution)/shard_map/pallas_call | solution.py:81
  200.4 7.2 %fusion.38 = bf16[128,8,128]{2,0,1:T(8,128)(2,1)S(1)} fusion(f32[1024,128,8]{1,0,2:T(8,128)} %fusion.59, bf16[1024,128]{1,0:T(8,128)(2,1)S(1)} %get-tuple-element.39, f32[8,128,1024]{1,2,0:T(8,128)} %get-tuple-element.67, f32[8,128]{1,0:T(8,128)S(1)} %get-tuple-element.66), kind=kOutput, calls=%fused_computation.52 | convolution fusion | flops 275908608 | bytes 8916992 | tf_op jit(solution)/shard_map/hts,sd->thd/dot_general | solution.py:364
  207.6 0.8 copy.46
  208.5 0.6 reduce_sum.67
  209.8 3.9 %convolution_convert_fusion.1 = bf16[512,1024]{1,0:T(8,128)(2,1)} fusion(bf16[1024,512]{1,0:T(8,128)(2,1)S(1)} %get-tuple-element.37, bf16[1024,1024]{0,1:T(8,128)(2,1)} %all-gather.7.cloned.1.call-done), kind=kOutput, calls=%fused_computation.43 | convolution fusion | flops 1074266112 | bytes 4194304 | tf_op jit(solution)/shard_map/dot_general | solution.py:372
  213.7 5.5 %fusion.31 = bf16[8,128,896]{2,1,0:T(8,128)(2,1)} fusion(bf16[8,1024,128]{2,1,0:T(8,128)(2,1)} %bitcast.125, bf16[256,896]{1,0:T(8,128)(2,1)} %collective-permute-done.5, bf16[256,896]{1,0:T(8,128)(2,1)} %copy-done.13, bf16[256,896]{1,0:T(8,128)(2,1)S(1)} %copy-done.12, bf16[256,896]{1,0:T(8,128)(2,1)S(1)} %copy-done.10), kind=kOutput, calls=%fused_computation.42 | convolution fusion | flops 1887305728 | bytes 5767168 | tf_op jit(solution)/shard_map/dot_general | solution.py:377
  219.3 5.2 %fusion.30 = bf16[8,128,896]{2,1,0:T(8,128)(2,1)} fusion(bf16[8,1024,128]{2,1,0:T(8,128)(2,1)S(1)} %bitcast.126, bf16[256,896]{1,0:T(8,128)(2,1)} %collective-permute-done.8, bf16[256,896]{1,0:T(8,128)(2,1)} %collective-permute-done.7, bf16[256,896]{1,0:T(8,128)(2,1)} %collective-permute-done.6, bf16[256,896]{1,0:T(8,128)(2,1)} %get-tuple-element.36), kind=kOutput, calls=%fused_computation.41 | convolution fusion | flops 1887305728 | bytes 5767168 | tf_op jit(solution)/shard_map/dot_general | solution.py:377
  224.5 1.3 copy.64
  (62 shorter events, 1.6 us)
Async XLA Ops:
  7.2 153.2 %copy-start = (bf16[512,1024]{1,0:T(8,128)(2,1)S(1)}, bf16[512,1024]{1,0:T(8,128)(2,1)}, u32[]{:S(2)}) copy-start(bf16[512,1024]{1,0:T(8,128)(2,1)} %param.17) | copy-start | bytes 3145732
  7.2 202.6 %all-gather.7.cloned.1.call-start = ((), (), s32[]{:S(2)}) async-start(), calls=%async_computation.1 | async-start | bytes 2359296 | tf_op jit(solution)/shard_map/all_gather | solution.py:356
  8.4 0.8 copy-start.2
  9.2 0.8 copy-start.3
  24.7 5.7 %copy-start.6 = (f32[4096]{0:T(1024)S(1)}, f32[4096]{0:T(1024)}, u32[]{:S(2)}) copy-start(f32[4096]{0:T(1024)} %param.12) | copy-start | bytes 49156
  28.0 4.9 %copy-start.8 = (bf16[256,896]{1,0:T(8,128)(2,1)S(1)}, bf16[256,896]{1,0:T(8,128)(2,1)}, u32[]{:S(2)}) copy-start(bf16[256,896]{1,0:T(8,128)(2,1)} %param.15) | copy-start | bytes 1376260
  28.1 185.6 %all-gather.5.cloned.1.call-start = ((), (), s32[]{:S(2)}) async-start(), calls=%async_computation | async-start | bytes 2359296 | tf_op jit(solution)/shard_map/all_gather | solution.py:336
  30.4 9.8 %slice-start = ((s8[7340032]{0:T(1024)(128)(4,1)}), s8[4194304]{0:T(1024)(128)(4,1)S(1)}, s32[]{:S(2)}) async-start(s8[7340032]{0:T(1024)(128)(4,1)} %bitcast.115), calls=%async_computation.3 | async-start | bytes 8388608
  32.9 7.2 %copy-start.4 = (bf16[256,4096]{1,0:T(8,128)(2,1)}, bf16[256,4096]{1,0:T(8,128)(2,1)S(1)}, u32[]{:S(2)}) copy-start(bf16[256,4096]{1,0:T(8,128)(2,1)S(1)} %fusion.5) | copy-start | bytes 6291460
  32.9 7.2 %slice-start.1 = ((s8[7340032]{0:T(1024)(128)(4,1)}), s8[3145728]{0:T(1024)(128)(4,1)S(1)}, s32[]{:S(2)}) async-start(s8[7340032]{0:T(1024)(128)(4,1)} %bitcast.115), calls=%async_computation.4 | async-start | bytes 6291456
  32.9 9.7 %slice-start.2 = ((s8[7340032]{0:T(1024)(128)(4,1)}), s8[4194304]{0:T(1024)(128)(4,1)S(1)}, s32[]{:S(2)}) async-start(s8[7340032]{0:T(1024)(128)(4,1)} %bitcast.123), calls=%async_computation.5 | async-start | bytes 8388608
  40.2 2.5 %slice-start.3 = ((s8[7340032]{0:T(1024)(128)(4,1)}), s8[3145728]{0:T(1024)(128)(4,1)S(1)}, s32[]{:S(2)}) async-start(s8[7340032]{0:T(1024)(128)(4,1)} %bitcast.123), calls=%async_computation.6 | async-start | bytes 6291456
  42.7 46.4 %copy-start.9 = (bf16[256,896]{1,0:T(8,128)(2,1)}, bf16[256,896]{1,0:T(8,128)(2,1)S(1)}, u32[]{:S(2)}) copy-start(bf16[256,896]{1,0:T(8,128)(2,1)S(1)} %fusion.34) | copy-start | bytes 1376260
  75.3 138.4 %all-gather.9.cloned.1.call-start = ((), (), s32[]{:S(2)}) async-start(), calls=%async_computation.2 | async-start | bytes 2359296 | tf_op jit(solution)/shard_map/all_gather | solution.py:311
  76.4 4.5 %collective-permute-start = (bf16[256,128]{1,0:T(8,128)(2,1)S(1)}, bf16[256,128]{1,0:T(8,128)(2,1)S(1)}, u32[]{:S(2)}, u32[]{:S(2)}) collective-permute-start(bf16[256,128]{1,0:T(8,128)(2,1)S(1)} %get-tuple-element.60), channel_id=1, source_target_pairs={{0,8},{8,16},{16,24},{24,0},{1,9},{9,17},{17,25},{25,1},{2,10},{10... | collective-permute-start | bytes 196616 | tf_op jit(solution)/shard_map/ppermute | solution.py:246
  77.9 6.0 %collective-permute-start.1 = (bf16[256,128]{1,0:T(8,128)(2,1)S(1)}, bf16[256,128]{1,0:T(8,128)(2,1)S(1)}, u32[]{:S(2)}, u32[]{:S(2)}) collective-permute-start(bf16[256,128]{1,0:T(8,128)(2,1)S(1)} %get-tuple-element.59), channel_id=1, source_target_pairs={{0,16},{8,24},{16,0},{24,8},{1,17},{9,25},{17,1},{25,9},{2,18},{10... | collective-permute-start | bytes 196616 | tf_op jit(solution)/shard_map/ppermute | solution.py:246
  79.3 6.3 %collective-permute-start.2 = (bf16[256,128]{1,0:T(8,128)(2,1)S(1)}, bf16[256,128]{1,0:T(8,128)(2,1)S(1)}, u32[]{:S(2)}, u32[]{:S(2)}) collective-permute-start(bf16[256,128]{1,0:T(8,128)(2,1)S(1)} %get-tuple-element.58), channel_id=1, source_target_pairs={{0,24},{8,0},{16,8},{24,16},{1,25},{9,1},{17,9},{25,17},{2,26},{10... | collective-permute-start | bytes 196616 | tf_op jit(solution)/shard_map/ppermute | solution.py:246
  86.4 13.4 %collective-permute-start.3 = (bf16[256,896]{1,0:T(8,128)(2,1)S(1)}, bf16[256,896]{1,0:T(8,128)(2,1)S(1)}, u32[]{:S(2)}, u32[]{:S(2)}) collective-permute-start(bf16[256,896]{1,0:T(8,128)(2,1)S(1)} %fusion.34), channel_id=1, source_target_pairs={{0,8},{8,16},{16,24},{24,0},{1,9},{9,17},{17,25},{25,1},{2,10},{10... | collective-permute-start | bytes 1376264 | tf_op jit(solution)/shard_map/ppermute | solution.py:246
  86.5 39.7 %collective-permute-start.4 = (bf16[256,896]{1,0:T(8,128)(2,1)S(1)}, bf16[256,896]{1,0:T(8,128)(2,1)S(1)}, u32[]{:S(2)}, u32[]{:S(2)}) collective-permute-start(bf16[256,896]{1,0:T(8,128)(2,1)S(1)} %fusion.34), channel_id=1, source_target_pairs={{0,16},{8,24},{16,0},{24,8},{1,17},{9,25},{17,1},{25,9},{2,18},{10... | collective-permute-start | bytes 1376264 | tf_op jit(solution)/shard_map/ppermute | solution.py:246
  89.1 39.7 %collective-permute-start.5 = (bf16[256,896]{1,0:T(8,128)(2,1)S(1)}, bf16[256,896]{1,0:T(8,128)(2,1)}, u32[]{:S(2)}, u32[]{:S(2)}) collective-permute-start(bf16[256,896]{1,0:T(8,128)(2,1)S(1)} %fusion.34), channel_id=1, source_target_pairs={{0,24},{8,0},{16,8},{24,16},{1,25},{9,1},{17,9},{25,17},{2,26},{10... | collective-permute-start | bytes 1376264 | tf_op jit(solution)/shard_map/ppermute | solution.py:246
  99.8 26.3 %copy-start.11 = (bf16[256,896]{1,0:T(8,128)(2,1)}, bf16[256,896]{1,0:T(8,128)(2,1)S(1)}, u32[]{:S(2)}) copy-start(bf16[256,896]{1,0:T(8,128)(2,1)S(1)} %collective-permute-done.3) | copy-start | bytes 1376260
  126.1 0.8 copy-start.13
  128.9 1.0 copy-start.1
  156.6 62.7 %collective-permute-start.6 = (bf16[256,896]{1,0:T(8,128)(2,1)}, bf16[256,896]{1,0:T(8,128)(2,1)}, u32[]{:S(2)}, u32[]{:S(2)}) collective-permute-start(bf16[256,896]{1,0:T(8,128)(2,1)} %get-tuple-element.36), channel_id=1, source_target_pairs={{0,8},{8,16},{16,24},{24,0},{1,9},{9,17},{17,25},{25,1},{2,10},{10... | collective-permute-start | bytes 1376264 | tf_op jit(solution)/shard_map/ppermute | solution.py:246
  157.2 62.0 %collective-permute-start.7 = (bf16[256,896]{1,0:T(8,128)(2,1)}, bf16[256,896]{1,0:T(8,128)(2,1)}, u32[]{:S(2)}, u32[]{:S(2)}) collective-permute-start(bf16[256,896]{1,0:T(8,128)(2,1)} %get-tuple-element.36), channel_id=1, source_target_pairs={{0,16},{8,24},{16,0},{24,8},{1,17},{9,25},{17,1},{25,9},{2,18},{10... | collective-permute-start | bytes 1376264 | tf_op jit(solution)/shard_map/ppermute | solution.py:246
  160.3 59.0 %collective-permute-start.8 = (bf16[256,896]{1,0:T(8,128)(2,1)}, bf16[256,896]{1,0:T(8,128)(2,1)}, u32[]{:S(2)}, u32[]{:S(2)}) collective-permute-start(bf16[256,896]{1,0:T(8,128)(2,1)} %get-tuple-element.36), channel_id=1, source_target_pairs={{0,24},{8,0},{16,8},{24,16},{1,25},{9,1},{17,9},{25,17},{2,26},{10... | collective-permute-start | bytes 1376264 | tf_op jit(solution)/shard_map/ppermute | solution.py:246
  209.7 4.0 %copy-start.10 = (bf16[256,896]{1,0:T(8,128)(2,1)S(1)}, bf16[256,896]{1,0:T(8,128)(2,1)}, u32[]{:S(2)}) copy-start(bf16[256,896]{1,0:T(8,128)(2,1)} %copy-done.9) | copy-start | bytes 1376260
  209.7 4.0 %copy-start.12 = (bf16[256,896]{1,0:T(8,128)(2,1)S(1)}, bf16[256,896]{1,0:T(8,128)(2,1)}, u32[]{:S(2)}) copy-start(bf16[256,896]{1,0:T(8,128)(2,1)} %copy-done.11) | copy-start | bytes 1376260
  213.7 5.6 %copy-start.7 = (bf16[8192,128]{1,0:T(8,128)(2,1)S(1)}, bf16[8192,128]{1,0:T(8,128)(2,1)}, u32[]{:S(2)}) copy-start(bf16[8192,128]{1,0:T(8,128)(2,1)} %all-gather.9.cloned.1.call-done) | copy-start | bytes 6291460
  219.3 5.2 %copy-start.5 = (bf16[256,4096]{1,0:T(8,128)(2,1)S(1)}, bf16[256,4096]{1,0:T(8,128)(2,1)}, u32[]{:S(2)}) copy-start(bf16[256,4096]{1,0:T(8,128)(2,1)} %all-gather.5.cloned.1.call-done) | copy-start | bytes 6291460
Sparse Core Ops, SparseCore 0:
  28.2 36.0 all-gather.6
  75.5 28.1 all-gather.4
  106.1 27.8 all-gather.8

commit v4 on v3

--- a/solution.py
+++ b/solution.py
@@ -32,6 +32,10 @@
     if dim == 0:
         return ref.at[pl.ds(start, size)]
     return ref.at[:, pl.ds(start, size)]
+
+
+def moved(nbytes):
+    return pl.CostEstimate(flops=0, bytes_accessed=nbytes, transcendentals=0)
 
 
 def params(collective_id):
@@ -90,6 +94,7 @@
             pltpu.SemaphoreType.DMA,
         ],
         compiler_params=params(collective_id),
+        cost_estimate=moved(32 * x.size * x.dtype.itemsize),
     )(x)
 
 
@@ -179,6 +184,7 @@
             pltpu.SemaphoreType.DMA((n // 2,)),
         ],
         compiler_params=params(collective_id),
+        cost_estimate=moved(32 * x.size * x.dtype.itemsize),
     )(x)
 
 
@@ -239,6 +245,7 @@
         out_specs=[ANY] * len(arrays),
         scratch_shapes=scratch,
         compiler_params=params(collective_id),
+        cost_estimate=moved(sum(96 * x.size * x.dtype.itemsize for x in arrays) + (1 << 24)),
     )(*arrays)
 
 
@@ -304,12 +311,11 @@
     partial_norm = partial_norm + lax.dot_general(
         grad_u, w_up, contract_last, preferred_element_type=jnp.float32
     )
-    gate_send, normed_parts = lax.optimization_barrier((grad_g, normed_parts))
-    gate_parts = [grad_g]
-    for k in range(1, heads_n):
-        gate_parts.append(shifted(gate_send, "head", heads_n, k))
+    partial_norm, normed_parts = lax.optimization_barrier(
+        (partial_norm.astype(jnp.bfloat16), normed_parts)
+    )
     normed_all = lax.all_gather(jnp.concatenate(normed_parts, axis=0), "wide", axis=0)
-    grad_norm = pair_scatter_sum(partial_norm.astype(jnp.bfloat16), "wide", 1, 1)
+    grad_norm = pair_scatter_sum(partial_norm, "wide", 1, 1)
     grad_norm = grad_norm.astype(jnp.float32)
     resid_own = lax.dynamic_slice_in_dim(residual, wide_at * cols_wide, cols_wide, 1)
     normed_own = resid_own.astype(jnp.float32) * inv_rms
@@ -326,12 +332,15 @@
     resid_grad = (
         out_own.astype(jnp.float32) + inv_rms * (grad_norm * gain_own - normed_own * mean_term)
     ).astype(jnp.bfloat16)
-    resid_send, gate_parts = lax.optimization_barrier((resid_grad, gate_parts))
-    resid_cols, gain_all = gather([resid_send, gain_part], [("head", 0), ("head", 0)], 3)
-    up_send, resid_cols = lax.optimization_barrier((grad_u, resid_cols))
-    up_parts = [grad_u]
+    resid_cols, gain_all = gather([resid_grad, gain_part], [("head", 0), ("head", 0)], 3)
+    grads_send, resid_cols = lax.optimization_barrier(
+        (jnp.concatenate([grad_g, grad_u], axis=0), resid_cols)
+    )
+    gate_parts, up_parts = [grad_g], [grad_u]
     for k in range(1, heads_n):
-        up_parts.append(shifted(up_send, "head", heads_n, k))
+        moved_in = shifted(grads_send, "head", heads_n, k)
+        gate_parts.append(moved_in[:tok_mlp])
+        up_parts.append(moved_in[tok_mlp:])
     grad_gain = jnp.sum(gain_all.reshape(heads_n, width), axis=0)
     grad_resid = lax.all_gather(resid_grad, "wide", axis=1, tiled=True)
 

time: 236 us -> 237 us (level); the launches traced: 232 us -> 236 us
  Pallas kernels: 85.5 us -> 92.7 us
  waiting for transfers between devices: 42.8 us -> 35.6 us
  local copies, waits for them, and re-layouts: 9.36 us -> 16.1 us
  starting transfers between devices: 12.3 us -> 8.67 us
    ppermute x9 -> x6, waiting for transfers between devices: 42.7 us -> 35.6 us  [shifted(): return lax.ppermute(x, axis, [(i, (i + k) % n) for i in range(n)])]
    slice x0 -> x3, local copies, waits for them, and re-layouts: none -> 6.54 us  [local(): up_parts.append(moved_in[tok_mlp:])]
    pallas_call x1, Pallas kernels: 8.61 us -> 13.3 us  [scatter_sum(): pl.pallas_call(functools.partial(scatter_sum_kernel, axis, n, dim), out_s...]
    ppermute x9 -> x6, starting transfers between devices: 12 us -> 8.36 us  [shifted(): return lax.ppermute(x, axis, [(i, (i + k) % n) for i in range(n)])]
    pallas_call x3, Pallas kernels: 41.2 us -> 43.6 us  [gather(): pl.pallas_call(functools.partial(gather_kernel, plan), out_shape=outs, in...]
    unnamed x38 -> x54, local copies, waits for them, and re-layouts: 5.5 us -> 6.55 us
  transfers between devices with their start and end apart: 12 -> 9, of which waited for: 5 -> 2; matrix products, arithmetic and copies ran while one was open for 25% -> 30% of each run, Pallas kernels for 33% -> 35%
where the time goes in v4:
time: 237 us; the launch traced here: 236 us
  Pallas kernels  92.7 us (39%)
  matrix products  56.7 us (24%)
  waiting for transfers between devices  35.6 us (15%)
  local copies, waits for them, and re-layouts  16.1 us (7%)
  between operations  14.2 us (6%)
  other arithmetic  12.3 us (5%)
  starting transfers between devices  8.67 us (4%)
    pallas_call x3, Pallas kernels, gather(): pl.pallas_call(functools.partial(gather_kernel, plan), out_shape=outs, in...  43.6 us
    pallas_call x2, Pallas kernels, pair_scatter_sum(): pl.pallas_call(functools.partial(pair_scatter_kernel, axis, n, dim), out_...  35.8 us
    ppermute x6, waiting for transfers between devices, shifted(): return lax.ppermute(x, axis, [(i, (i + k) % n) for i in range(n)])  35.6 us
    pallas_call x1, Pallas kernels, scatter_sum(): pl.pallas_call(functools.partial(scatter_sum_kernel, axis, n, dim), out_s...  13.3 us
    dot_general x2, matrix products, local(): lax.dot_general(normed_all, jnp.concatenate(parts, axis=0), contract_toke...  9.03 us
    ppermute x6, starting transfers between devices, shifted(): return lax.ppermute(x, axis, [(i, (i + k) % n) for i in range(n)])  8.36 us
    dot_general x1, matrix products, local(): jnp.einsum('hts,sd->thd', dscore, keys_all, preferred_element_type=jnp.fl...  8.04 us
    dot_general x1, matrix products, local(): jnp.einsum('hts,thd->sd', dscore, query3, preferred_element_type=jnp.floa...  7.82 us
  transfers between devices with their start and end apart: 9, of which 2 were waited for; matrix products, arithmetic and copies ran while one was open for 30% of the time, Pallas kernels for 35%

profile of v4, /device:TPU:8, one launch (start us, length us, event | category | flops | bytes accessed | tf_op | source)
XLA Modules:
  0.0 236.4 jit_solution(7041824777328879119)
XLA Ops:
  7.2 1.2 copy.61
  8.5 0.8 copy-done.4
  9.2 0.8 copy-done.5
  10.0 9.7 %shard_map.173 = (bf16[1024,128]{1,0:T(8,128)(2,1)S(1)}, bf16[1024,128]{1,0:T(8,128)(2,1)S(1)}) custom-call(bf16[128,128]{1,0:T(8,128)(2,1)S(1)} %copy-done.4, bf16[128,128]{1,0:T(8,128)(2,1)S(1)} %copy-done.5), custom_call_target="tpu_custom_call" | custom-call | bytes 23068672 | tf_op jit(solution)/shard_map/pallas_call | solution.py:241
  19.7 0.8 dynamic_slice.31
  20.5 0.9 fusion.47
  21.4 3.4 %fusion.75 = (f32[8,128]{1,0:T(8,128)S(1)}, f32[8,128,1024]{1,2,0:T(8,128)}) fusion(pred[128,1024]{0,1:T(8,128)(4,1)S(1)} %fusion.47, bf16[128,8,128]{0,2,1:T(8,128)(2,1)S(1)} %bitcast.120, bf16[1024,128]{1,0:T(8,128)(2,1)S(1)} %get-tuple-element.29), kind=kOutput, calls=%fused_computation.105 | convolution fusion | flops 272630784 | bytes 4853760 | tf_op jit(solution)/shard_map/sub | solution.py:360
  24.7 3.4 %convolution_convert_fusion.2 = bf16[128,8,128]{2,0,1:T(8,128)(2,1)} fusion(bf16[1024,128]{1,0:T(8,128)(2,1)S(1)} %get-tuple-element.28, f32[8,128,1024]{1,2,0:T(8,128)} %get-tuple-element.63, f32[8,128]{1,0:T(8,128)S(1)} %get-tuple-element.62), kind=kOutput, calls=%fused_computation.53 | convolution fusion | flops 270663680 | bytes 4722688 | tf_op jit(solution)/shard_map/hts,sd->thd/dot_general | solution.py:363
  28.2 2.1 fusion.3
  30.3 2.2 fusion.5
  32.6 1.6 collective-permute-start
  34.3 1.2 collective-permute-start.1
  35.5 1.8 collective-permute-start.2
  37.3 6.2 %fusion.42 = (bf16[256,896]{1,0:T(8,128)(2,1)S(1)}, f32[256,896]{1,0:T(8,128)S(1)}) fusion(bf16[256,896]{1,0:T(8,128)(2,1)} %param.15, bf16[256,4096]{1,0:T(8,128)(2,1)S(1)} %fusion.5, bf16[4096,896]{1,0:T(8,128)(2,1)} %param.13), kind=kOutput, calls=%fused_computation.58 | convolution fusion | flops 1880653824 | bytes 11272192 | tf_op jit(solution)/shard_map/dot_general | solution.py:302
  43.6 2.5 %fusion.34 = bf16[256,896]{1,0:T(8,128)(2,1)S(1)} fusion(bf16[256,4096]{1,0:T(8,128)(2,1)S(1)} %fusion.5, bf16[4096,896]{1,0:T(8,128)(2,1)S(1)} %bitcast.116, bf16[256,896]{1,0:T(8,128)(2,1)S(1)} %copy-done.21, f32[256,896]{1,0:T(8,128)S(1)} %get-tuple-element.61), kind=kOutput, calls=%fused_computation.47 | convolution fusion | flops 1881571328 | bytes 11272192 | tf_op jit(solution)/shard_map/dot_general | solution.py:303
  46.2 2.4 %fusion.80 = f32[256,4096]{1,0:T(8,128)S(1)} fusion(bf16[256,896]{1,0:T(8,128)(2,1)S(1)} %fusion.34, bf16[4096,896]{1,0:T(8,128)(2,1)S(1)} %bitcast.124), kind=kOutput, calls=%fused_computation.106 | convolution fusion | flops 1879048192 | bytes 11993088 | tf_op jit(solution)/shard_map/dot_general | solution.py:308
  48.6 2.4 %fusion.2.src = bf16[256,4096]{1,0:T(8,128)(2,1)S(1)} fusion(f32[256,4096]{1,0:T(8,128)S(1)} %fusion.80, bf16[256,896]{1,0:T(8,128)(2,1)S(1)} %get-tuple-element.60, bf16[4096,896]{1,0:T(8,128)(2,1)S(1)} %bitcast.116), kind=kOutput, calls=%fused_computation.5 | convolution fusion | flops 1881145344 | bytes 14090240 | tf_op jit(solution)/shard_map/dot_general | solution.py:311
  51.0 0.7 pad_maximum_fusion.2
  51.7 0.2 all-gather.5.cloned.1.call-start
  52.0 2.2 pad_maximum_fusion
  54.2 18.7 %shard_map.170 = bf16[256,512]{1,0:T(8,128)(2,1)S(1)} custom-call(bf16[256,4096]{1,0:T(8,128)(2,1)S(1)} %fusion.2.src), custom_call_target="tpu_custom_call" | custom-call | bytes 67108864 | tf_op jit(solution)/shard_map/pallas_call | solution.py:172
  72.9 1.2 multiply_reduce_fusion
  74.2 5.6 %shard_map.171 = f32[64,128]{1,0:T(8,128)S(1)} custom-call(f32[8,128]{1,0:T(8,128)S(1)} %fusion.62.refs_0_), custom_call_target="tpu_custom_call" | custom-call | bytes 17170432 | tf_op jit(solution)/shard_map/pallas_call | solution.py:241
  79.9 1.2 fusion.46.refs_0_
  81.1 28.4 %shard_map.172 = (bf16[1024,512]{1,0:T(8,128)(2,1)S(1)}, f32[128,128]{1,0:T(8,128)S(1)}) custom-call(bf16[256,512]{1,0:T(8,128)(2,1)S(1)} %fusion.46.refs_0_, f32[32,128]{1,0:T(8,128)S(1)} %reshape.115.refs_1_), custom_call_target="tpu_custom_call" | custom-call | bytes 43515904 | tf_op jit(solution)/shard_map/pallas_call | solution.py:241
  109.5 1.3 convolution_convert_fusion.src
  110.8 17.1 %shard_map.174 = bf16[128,1024]{1,0:T(8,128)(2,1)S(1)} custom-call(bf16[1024,1024]{1,0:T(8,128)(2,1)S(1)} %convolution_convert_fusion.src), custom_call_target="tpu_custom_call" | custom-call | bytes 67108864 | tf_op jit(solution)/shard_map/pallas_call | solution.py:172
  127.9 0.2 copy.62
  128.1 0.4 collective-permute-start.3
  128.5 3.6 %fusion.36 = bf16[1024,128]{1,0:T(8,128)(2,1)} fusion(bf16[128,8,128]{0,2,1:T(8,128)(2,1)S(1)} %bitcast.117, f32[8,128,1024]{1,2,0:T(8,128)} %get-tuple-element.63, f32[8,128]{1,0:T(8,128)S(1)} %get-tuple-element.62), kind=kOutput, calls=%fused_computation.50 | convolution fusion | flops 270663680 | bytes 4722688 | tf_op jit(solution)/shard_map/hts,thd->sd/dot_general | solution.py:376
  132.1 2.7 %fusion.59 = f32[1024,128,8]{1,0,2:T(8,128)} fusion(bf16[128,8,128]{0,2,1:T(8,128)(2,1)S(1)} %bitcast.118, bf16[1024,128]{1,0:T(8,128)(2,1)S(1)} %copy-done.3), kind=kOutput, calls=%fused_computation.79 | convolution fusion | flops 268435456 | bytes 4718592 | tf_op jit(solution)/shard_map/thd,sd->hts/dot_general | solution.py:370
  134.9 3.3 %collective-permute-start.4 = (bf16[512,896]{1,0:T(8,128)(2,1)S(1)}, bf16[512,896]{1,0:T(8,128)(2,1)}, u32[]{:S(2)}, u32[]{:S(2)}) collective-permute-start(bf16[512,896]{1,0:T(8,128)(2,1)S(1)} %copy-done.10), channel_id=1, source_target_pairs={{0,16},{8,24},{16,0},{24,8},{1,17},{9,25},{17,1},{25,9},{2,18},{10... | collective-permute-start | bytes 2752520 | tf_op jit(solution)/shard_map/ppermute | solution.py:253
  138.2 7.8 %fusion.37 = bf16[1024,128]{1,0:T(8,128)(2,1)} fusion(bf16[128,8,128]{0,2,1:T(8,128)(2,1)} %bitcast.121, f32[1024,128,8]{1,0,2:T(8,128)} %fusion.59, f32[8,128,1024]{1,2,0:T(8,128)} %get-tuple-element.63, f32[8,128]{1,0:T(8,128)S(1)} %get-tuple-element.62), kind=kOutput, calls=%fused_computation.51 | convolution fusion | flops 275908608 | bytes 8916992 | tf_op jit(solution)/shard_map/hts,thd->sd/dot_general | solution.py:375
  146.0 1.1 pad_maximum_fusion.1.src
  147.1 13.3 %shard_map.175 = bf16[128,256]{1,0:T(8,128)(2,1)S(1)} custom-call(bf16[1024,256]{1,0:T(8,128)(2,1)S(1)} %pad_maximum_fusion.1.src), custom_call_target="tpu_custom_call" | custom-call | bytes 16777216 | tf_op jit(solution)/shard_map/pallas_call | solution.py:85
  160.4 8.0 %fusion.38 = bf16[128,8,128]{2,0,1:T(8,128)(2,1)} fusion(f32[1024,128,8]{1,0,2:T(8,128)} %fusion.59, bf16[1024,128]{1,0:T(8,128)(2,1)S(1)} %copy-done.7, f32[8,128,1024]{1,2,0:T(8,128)} %get-tuple-element.63, f32[8,128]{1,0:T(8,128)S(1)} %get-tuple-element.62), kind=kOutput, calls=%fused_computation.52 | convolution fusion | flops 275908608 | bytes 8916992 | tf_op jit(solution)/shard_map/hts,sd->thd/dot_general | solution.py:373
  168.4 1.8 copy.46
  170.2 0.6 reduce_sum.67
  170.9 0.6 fusion.74
  171.5 2.2 fusion.71
  173.7 33.8 %collective-permute-done.4 = bf16[512,896]{1,0:T(8,128)(2,1)} collective-permute-done((bf16[512,896]{1,0:T(8,128)(2,1)S(1)}, bf16[512,896]{1,0:T(8,128)(2,1)}, u32[]{:S(2)}, u32[]{:S(2)}) %collective-permute-start.4) | collective-permute-done | bytes 917536 | tf_op jit(solution)/shard_map/ppermute | solution.py:253
  207.5 2.2 fusion.72
  209.7 1.7 collective-permute-done.5
  211.4 2.2 fusion.73
  213.6 4.0 %convolution_convert_fusion.1 = bf16[512,1024]{1,0:T(8,128)(2,1)} fusion(bf16[1024,512]{1,0:T(8,128)(2,1)S(1)} %get-tuple-element.27, bf16[1024,1024]{0,1:T(8,128)(2,1)} %all-gather.7.cloned.1.call-done), kind=kOutput, calls=%fused_computation.43 | convolution fusion | flops 1074266112 | bytes 4194304 | tf_op jit(solution)/shard_map/dot_general | solution.py:381
  217.7 5.4 %fusion.30 = bf16[8,128,896]{2,1,0:T(8,128)(2,1)} fusion(bf16[8,1024,128]{2,1,0:T(8,128)(2,1)} %bitcast.125, bf16[256,896]{1,0:T(8,128)(2,1)} %get-tuple-element.56, bf16[256,896]{1,0:T(8,128)(2,1)S(1)} %copy-done.16, bf16[256,896]{1,0:T(8,128)(2,1)S(1)} %copy-done.15, bf16[256,896]{1,0:T(8,128)(2,1)S(1)} %copy-done.9), kind=kOutput, calls=%fused_computation.41 | convolution fusion | flops 1887305728 | bytes 5767168 | tf_op jit(solution)/shard_map/dot_general | solution.py:386
  223.1 3.6 %fusion.31 = bf16[8,128,896]{2,1,0:T(8,128)(2,1)} fusion(bf16[8,1024,128]{2,1,0:T(8,128)(2,1)S(1)} %bitcast.126, bf16[256,896]{1,0:T(8,128)(2,1)S(1)} %copy-done.17, bf16[256,896]{1,0:T(8,128)(2,1)S(1)} %copy-done.14, bf16[256,896]{1,0:T(8,128)(2,1)S(1)} %copy-done.13, bf16[256,896]{1,0:T(8,128)(2,1)S(1)} %copy-done.12), kind=kOutput, calls=%fused_computation.42 | convolution fusion | flops 1887305728 | bytes 5767168 | tf_op jit(solution)/shard_map/dot_general | solution.py:386
  226.7 3.1 %copy.64 = bf16[256,4096]{1,0:T(8,128)(2,1)} copy(bf16[256,4096]{1,0:T(8,128)(2,1)} %all-gather.5.cloned.1.call-done) | data formatting | bytes 4194304
  (76 shorter events, 0.5 us)
Async XLA Ops:
  7.2 102.3 %copy-start = (bf16[512,1024]{1,0:T(8,128)(2,1)S(1)}, bf16[512,1024]{1,0:T(8,128)(2,1)}, u32[]{:S(2)}) copy-start(bf16[512,1024]{1,0:T(8,128)(2,1)} %param.17) | copy-start | bytes 3145732
  7.2 206.4 %all-gather.7.cloned.1.call-start = ((), (), s32[]{:S(2)}) async-start(), calls=%async_computation.1 | async-start | bytes 2359296 | tf_op jit(solution)/shard_map/all_gather | solution.py:365
  8.4 0.8 copy-start.4
  9.2 0.8 copy-start.5
  10.0 18.1 %copy-start.18 = (bf16[128,1024]{0,1:T(8,128)(2,1)}, bf16[128,1024]{0,1:T(8,128)(2,1)S(1)}, u32[]{:S(2)}) copy-start(bf16[128,1024]{0,1:T(8,128)(2,1)S(1)} %copy.61) | copy-start | bytes 786436
  19.7 8.5 %copy-start.2 = (bf16[1024,128]{1,0:T(8,128)(2,1)}, bf16[1024,128]{1,0:T(8,128)(2,1)S(1)}, u32[]{:S(2)}) copy-start(bf16[1024,128]{1,0:T(8,128)(2,1)S(1)} %get-tuple-element.28) | copy-start | bytes 786436
  19.7 8.5 %copy-start.6 = (bf16[1024,128]{1,0:T(8,128)(2,1)}, bf16[1024,128]{1,0:T(8,128)(2,1)S(1)}, u32[]{:S(2)}) copy-start(bf16[1024,128]{1,0:T(8,128)(2,1)S(1)} %get-tuple-element.29) | copy-start | bytes 786436
  24.7 5.5 %copy-start.19 = (f32[4096]{0:T(1024)S(1)}, f32[4096]{0:T(1024)}, u32[]{:S(2)}) copy-start(f32[4096]{0:T(1024)} %param.12) | copy-start | bytes 49156
  28.1 189.5 %all-gather.9.cloned.1.call-start = ((), (), s32[]{:S(2)}) async-start(), calls=%async_computation.2 | async-start | bytes 2359296 | tf_op jit(solution)/shard_map/all_gather | solution.py:317
  32.6 18.3 %collective-permute-start = (bf16[256,128]{1,0:T(8,128)(2,1)S(1)}, bf16[256,128]{1,0:T(8,128)(2,1)S(1)}, u32[]{:S(2)}, u32[]{:S(2)}) collective-permute-start(bf16[256,128]{1,0:T(8,128)(2,1)S(1)} %get-tuple-element.50), channel_id=1, source_target_pairs={{0,8},{8,16},{16,24},{24,0},{1,9},{9,17},{17,25},{25,1},{2,10},{10... | collective-permute-start | bytes 196616 | tf_op jit(solution)/shard_map/ppermute | solution.py:253
  34.3 16.7 %collective-permute-start.1 = (bf16[256,128]{1,0:T(8,128)(2,1)S(1)}, bf16[256,128]{1,0:T(8,128)(2,1)S(1)}, u32[]{:S(2)}, u32[]{:S(2)}) collective-permute-start(bf16[256,128]{1,0:T(8,128)(2,1)S(1)} %get-tuple-element.49), channel_id=1, source_target_pairs={{0,16},{8,24},{16,0},{24,8},{1,17},{9,25},{17,1},{25,9},{2,18},{10... | collective-permute-start | bytes 196616 | tf_op jit(solution)/shard_map/ppermute | solution.py:253
  35.5 8.1 %slice-start = ((s8[7340032]{0:T(1024)(128)(4,1)}), s8[4194304]{0:T(1024)(128)(4,1)S(1)}, s32[]{:S(2)}) async-start(s8[7340032]{0:T(1024)(128)(4,1)} %bitcast.115), calls=%async_computation.3 | async-start | bytes 8388608
  35.5 8.1 %slice-start.1 = ((s8[7340032]{0:T(1024)(128)(4,1)}), s8[3145728]{0:T(1024)(128)(4,1)S(1)}, s32[]{:S(2)}) async-start(s8[7340032]{0:T(1024)(128)(4,1)} %bitcast.115), calls=%async_computation.4 | async-start | bytes 6291456
  35.5 8.1 %copy-start.21 = (bf16[256,896]{1,0:T(8,128)(2,1)S(1)}, bf16[256,896]{1,0:T(8,128)(2,1)}, u32[]{:S(2)}) copy-start(bf16[256,896]{1,0:T(8,128)(2,1)} %param.15) | copy-start | bytes 1376260
  35.5 15.5 %collective-permute-start.2 = (bf16[256,128]{1,0:T(8,128)(2,1)S(1)}, bf16[256,128]{1,0:T(8,128)(2,1)S(1)}, u32[]{:S(2)}, u32[]{:S(2)}) collective-permute-start(bf16[256,128]{1,0:T(8,128)(2,1)S(1)} %get-tuple-element.48), channel_id=1, source_target_pairs={{0,24},{8,0},{16,8},{24,16},{1,25},{9,1},{17,9},{25,17},{2,26},{10... | collective-permute-start | bytes 196616 | tf_op jit(solution)/shard_map/ppermute | solution.py:253
  37.3 8.8 %slice-start.2 = ((s8[7340032]{0:T(1024)(128)(4,1)}), s8[4194304]{0:T(1024)(128)(4,1)S(1)}, s32[]{:S(2)}) async-start(s8[7340032]{0:T(1024)(128)(4,1)} %bitcast.123), calls=%async_computation.5 | async-start | bytes 8388608
  43.5 5.0 %copy-start.8 = (bf16[256,896]{1,0:T(8,128)(2,1)}, bf16[256,896]{1,0:T(8,128)(2,1)S(1)}, u32[]{:S(2)}) copy-start(bf16[256,896]{1,0:T(8,128)(2,1)S(1)} %get-tuple-element.60) | copy-start | bytes 1376260
  43.6 2.5 %slice-start.3 = ((s8[7340032]{0:T(1024)(128)(4,1)}), s8[3145728]{0:T(1024)(128)(4,1)S(1)}, s32[]{:S(2)}) async-start(s8[7340032]{0:T(1024)(128)(4,1)} %bitcast.123), calls=%async_computation.6 | async-start | bytes 6291456
  46.1 2.4 %copy-start.11 = (bf16[256,896]{1,0:T(8,128)(2,1)}, bf16[256,896]{1,0:T(8,128)(2,1)S(1)}, u32[]{:S(2)}) copy-start(bf16[256,896]{1,0:T(8,128)(2,1)S(1)} %fusion.34) | copy-start | bytes 1376260
  51.7 175.0 %all-gather.5.cloned.1.call-start = ((), (), s32[]{:S(2)}) async-start(), calls=%async_computation | async-start | bytes 2359296 | tf_op jit(solution)/shard_map/all_gather | solution.py:345
  81.1 29.6 %copy-start.1 = (bf16[256,512]{1,0:T(8,128)(2,1)}, bf16[256,512]{1,0:T(8,128)(2,1)S(1)}, u32[]{:S(2)}) copy-start(bf16[256,512]{1,0:T(8,128)(2,1)S(1)} %fusion.46.refs_0_) | copy-start | bytes 786436
  128.1 43.4 %collective-permute-start.3 = (bf16[512,896]{1,0:T(8,128)(2,1)}, bf16[512,896]{1,0:T(8,128)(2,1)}, u32[]{:S(2)}, u32[]{:S(2)}) collective-permute-start(bf16[512,896]{1,0:T(8,128)(2,1)} %pad_maximum_fusion), channel_id=1, source_target_pairs={{0,8},{8,16},{16,24},{24,0},{1,9},{9,17},{17,25},{25,1},{2,10},{10... | collective-permute-start | bytes 2752520 | tf_op jit(solution)/shard_map/ppermute | solution.py:253
  128.5 3.7 %copy-start.3 = (bf16[1024,128]{1,0:T(8,128)(2,1)S(1)}, bf16[1024,128]{1,0:T(8,128)(2,1)}, u32[]{:S(2)}) copy-start(bf16[1024,128]{1,0:T(8,128)(2,1)} %copy-done.2) | copy-start | bytes 786436
  132.1 2.7 %copy-start.10 = (bf16[512,896]{1,0:T(8,128)(2,1)S(1)}, bf16[512,896]{1,0:T(8,128)(2,1)}, u32[]{:S(2)}) copy-start(bf16[512,896]{1,0:T(8,128)(2,1)} %pad_maximum_fusion) | copy-start | bytes 2752516
  134.9 25.5 %copy-start.7 = (bf16[1024,128]{1,0:T(8,128)(2,1)S(1)}, bf16[1024,128]{1,0:T(8,128)(2,1)}, u32[]{:S(2)}) copy-start(bf16[1024,128]{1,0:T(8,128)(2,1)} %copy-done.6) | copy-start | bytes 786436
  134.9 72.6 %collective-permute-start.4 = (bf16[512,896]{1,0:T(8,128)(2,1)S(1)}, bf16[512,896]{1,0:T(8,128)(2,1)}, u32[]{:S(2)}, u32[]{:S(2)}) collective-permute-start(bf16[512,896]{1,0:T(8,128)(2,1)S(1)} %copy-done.10), channel_id=1, source_target_pairs={{0,16},{8,24},{16,0},{24,8},{1,17},{9,25},{17,1},{25,9},{2,18},{10... | collective-permute-start | bytes 2752520 | tf_op jit(solution)/shard_map/ppermute | solution.py:253
  138.2 73.2 %collective-permute-start.5 = (bf16[512,896]{1,0:T(8,128)(2,1)S(1)}, bf16[512,896]{1,0:T(8,128)(2,1)}, u32[]{:S(2)}, u32[]{:S(2)}) collective-permute-start(bf16[512,896]{1,0:T(8,128)(2,1)S(1)} %copy-done.10), channel_id=1, source_target_pairs={{0,24},{8,0},{16,8},{24,16},{1,25},{9,1},{17,9},{25,17},{2,26},{10... | collective-permute-start | bytes 2752520 | tf_op jit(solution)/shard_map/ppermute | solution.py:253
  213.6 4.0 %copy-start.9 = (bf16[256,896]{1,0:T(8,128)(2,1)S(1)}, bf16[256,896]{1,0:T(8,128)(2,1)}, u32[]{:S(2)}) copy-start(bf16[256,896]{1,0:T(8,128)(2,1)} %copy-done.8) | copy-start | bytes 1376260
  213.6 4.0 %copy-start.15 = (bf16[256,896]{1,0:T(8,128)(2,1)S(1)}, bf16[256,896]{1,0:T(8,128)(2,1)}, u32[]{:S(2)}) copy-start(bf16[256,896]{1,0:T(8,128)(2,1)} %get-tuple-element.52) | copy-start | bytes 1376260
  213.6 4.0 %copy-start.16 = (bf16[256,896]{1,0:T(8,128)(2,1)S(1)}, bf16[256,896]{1,0:T(8,128)(2,1)}, u32[]{:S(2)}) copy-start(bf16[256,896]{1,0:T(8,128)(2,1)} %get-tuple-element.54) | copy-start | bytes 1376260
  217.6 5.5 %copy-start.12 = (bf16[256,896]{1,0:T(8,128)(2,1)S(1)}, bf16[256,896]{1,0:T(8,128)(2,1)}, u32[]{:S(2)}) copy-start(bf16[256,896]{1,0:T(8,128)(2,1)} %copy-done.11) | copy-start | bytes 1376260
  217.6 5.5 %copy-start.13 = (bf16[256,896]{1,0:T(8,128)(2,1)S(1)}, bf16[256,896]{1,0:T(8,128)(2,1)}, u32[]{:S(2)}) copy-start(bf16[256,896]{1,0:T(8,128)(2,1)} %get-tuple-element.53) | copy-start | bytes 1376260
  217.6 5.4 %copy-start.14 = (bf16[256,896]{1,0:T(8,128)(2,1)S(1)}, bf16[256,896]{1,0:T(8,128)(2,1)}, u32[]{:S(2)}) copy-start(bf16[256,896]{1,0:T(8,128)(2,1)} %get-tuple-element.55) | copy-start | bytes 1376260
  217.6 5.4 %copy-start.17 = (bf16[256,896]{1,0:T(8,128)(2,1)S(1)}, bf16[256,896]{1,0:T(8,128)(2,1)}, u32[]{:S(2)}) copy-start(bf16[256,896]{1,0:T(8,128)(2,1)} %get-tuple-element.57) | copy-start | bytes 1376260
  217.7 5.4 %copy-start.20 = (bf16[8192,128]{1,0:T(8,128)(2,1)S(1)}, bf16[8192,128]{1,0:T(8,128)(2,1)}, u32[]{:S(2)}) copy-start(bf16[8192,128]{1,0:T(8,128)(2,1)} %all-gather.9.cloned.1.call-done) | copy-start | bytes 6291460
Sparse Core Ops, SparseCore 0:
  28.3 29.3 all-gather.6
  59.5 28.0 all-gather.8
  128.6 35.3 all-gather.4
